TPU v7x, 128 devices: a whole 4x4x4 slice. The times are simulated.
128 devices in a mesh: dp: 8 (over z_hi, y), blk: 2 (over z_lo), ulysses: 8 (over x, core).
Axes of the slice: x: 4, y: 4, z: 4 (z_hi: 2, z_lo: 2; z = z_hi * 2 + z_lo), core: 2. Of those that a mesh axis runs over, the one named last changes fastest.
Arguments:
- video_query: bfloat16 [32768, 3072], P(('dp', 'blk', 'ulysses')), parts along dimension 0, may hold values from -20 to 20
- video_key: bfloat16 [32768, 3072], P(('dp', 'blk', 'ulysses')), parts along dimension 0, may hold values from -20 to 20
- video_value: bfloat16 [32768, 3072], P(('dp', 'blk', 'ulysses')), parts along dimension 0, may hold values from -6 to 6
- text_query: bfloat16 [2048, 3072], P(('dp', 'ulysses')), parts along dimension 0, may hold values from -20 to 20
- text_key: bfloat16 [2048, 3072], P(('dp', 'ulysses')), parts along dimension 0, may hold values from -6 to 6
- text_value: bfloat16 [2048, 3072], P(('dp', 'ulysses')), parts along dimension 0, may hold values from -6 to 6
- text_length: int32 [8], P('dp'), parts along dimension 0, may hold values from 64 to 256
Outputs:
- video_out: bfloat16 [32768, 3072], P(('dp', 'blk', 'ulysses')), parts along dimension 0
- text_out: bfloat16 [2048, 3072], P(('dp', 'blk', 'ulysses')), parts along dimension 0
There are 8 independent parts, one for each index of `dp`. A program takes and returns all parts, laid end to end along the dimension named above; each array names one. Nothing has to cross between parts.
All inputs are finite; a program needn't handle non-finite values.
Results may differ from a plain program's by a relative error of at most 0.009.
Values may be sent and summed in bfloat16 or wider, within the bound.
A program may use at most 128 MiB of HBM per device.

v0:
```python
import jax
import jax.numpy as jnp
from jax import lax
from jax.sharding import PartitionSpec as P

HEADS = 24


NEG_BIG = -1e30


def attend_block(carry, queries, keys, values, valid):
    top, total, summed = carry
    scale = queries.shape[-1] ** (-0.5)
    scores = jnp.einsum("qhd,khd->hqk", queries, keys, preferred_element_type=jnp.float32) * scale
    scores = jnp.where(valid[None, None, :], scores, jnp.float32(NEG_BIG))
    new_top = jnp.maximum(top, jnp.max(scores, axis=-1))
    factor = jnp.exp(top - new_top)
    weights = jnp.where(
        valid[None, None, :], jnp.exp(scores - new_top[..., None]), jnp.float32(0.0)
    )
    total = total * factor + jnp.sum(weights, axis=-1)
    summed = summed * factor[..., None] + jnp.einsum(
        "hqk,khd->hqd", weights.astype(jnp.bfloat16), values, preferred_element_type=jnp.float32
    )
    return (new_top, total, summed)


def attend_video(carry, queries, keys, values):
    count = keys.shape[0]
    width = 512
    blocks_k = keys.reshape(count // width, width, keys.shape[1], keys.shape[2])
    blocks_v = values.reshape(count // width, width, values.shape[1], values.shape[2])
    every = jnp.ones((width,), dtype=bool)

    def step(inner, pair):
        return (attend_block(inner, queries, pair[0], pair[1], every), None)

    carry, unused = lax.scan(step, carry, (blocks_k, blocks_v))
    return carry


def on_device(video_query, video_key, video_value, text_query, text_key, text_value, text_length):
    groups = lax.axis_size("ulysses")
    width = video_query.shape[1]
    heads_here = HEADS // groups
    head_size = width // HEADS
    moved = (
        lax.all_to_all(video_query, "ulysses", split_axis=1, concat_axis=0, tiled=True),
        lax.all_to_all(text_query, "ulysses", split_axis=1, concat_axis=0, tiled=True),
        lax.all_to_all(text_key, "ulysses", split_axis=1, concat_axis=0, tiled=True),
        lax.all_to_all(text_value, "ulysses", split_axis=1, concat_axis=0, tiled=True),
        lax.all_to_all(video_key, "ulysses", split_axis=1, concat_axis=0, tiled=True),
        lax.all_to_all(video_value, "ulysses", split_axis=1, concat_axis=0, tiled=True),
    )
    vq, tq, tk, tv, vk, vv = moved

    def split_heads(block):
        return block.reshape(block.shape[0], heads_here, head_size)

    queries = split_heads(jnp.concatenate([vq, tq], axis=0))
    rows = queries.shape[0]
    start = (
        jnp.full((heads_here, rows), NEG_BIG, jnp.float32),
        jnp.zeros((heads_here, rows), jnp.float32),
        jnp.zeros((heads_here, rows, head_size), jnp.float32),
    )
    carry = attend_video(
        start,
        queries,
        split_heads(lax.all_gather(vk, "blk", axis=0, tiled=True)),
        split_heads(lax.all_gather(vv, "blk", axis=0, tiled=True)),
    )
    text_valid = jnp.arange(tk.shape[0], dtype=jnp.int32) < text_length[0]
    top, total, summed = attend_block(carry, queries, split_heads(tk), split_heads(tv), text_valid)
    attended = (
        (summed / total[..., None])
        .transpose(1, 0, 2)
        .reshape(rows, heads_here * head_size)
        .astype(jnp.bfloat16)
    )
    video_rows = vq.shape[0]
    text_rows = attended[video_rows:]
    half_text = text_rows.shape[0] // lax.axis_size("blk")
    text_half = lax.dynamic_slice_in_dim(text_rows, lax.axis_index("blk") * half_text, half_text, 0)
    video_back, text_back = (
        lax.all_to_all(attended[:video_rows], "ulysses", split_axis=0, concat_axis=1, tiled=True),
        lax.all_to_all(text_half, "ulysses", split_axis=0, concat_axis=1, tiled=True),
    )
    return (video_back, text_back)


def solution(mesh):
    return jax.shard_map(
        on_device,
        mesh=mesh,
        in_specs=(
            P(("dp", "blk", "ulysses"), None),
            P(("dp", "blk", "ulysses"), None),
            P(("dp", "blk", "ulysses"), None),
            P(("dp", "ulysses"), None),
            P(("dp", "ulysses"), None),
            P(("dp", "ulysses"), None),
            P("dp"),
        ),
        out_specs=(P(("dp", "blk", "ulysses"), None), P(("dp", "blk", "ulysses"), None)),
        check_vma=False,
    )
```

profile of v0, /device:TPU:22, one launch (start us, length us, event | category | flops | bytes accessed | tf_op | source)
XLA Modules:
  0.0 428.5 jit_solution(18077896407698359581)
XLA Ops:
  7.2 1.7 copy.54
  8.9 24.3 %all_to_all.140 = bf16[256,8,384]{0,2,1:T(8,128)(2,1)S(1)} all-to-all(bf16[256,8,384]{0,2,1:T(8,128)(2,1)S(1)} %bitcast.82), channel_id=1, replica_groups=mesh['dp'=8,'blk'=2,'ulysses'=8] {'ulysses'}, dimensions={1} | all-to-all | bytes 3145728 | tf_op jit(solution)/shard_map/all_to_all | solution.py:53
  33.2 1.6 copy.55
  34.9 1.7 copy.62
  36.6 24.4 %all_to_all.141 = bf16[256,8,384]{0,2,1:T(8,128)(2,1)S(1)} all-to-all(bf16[256,8,384]{0,2,1:T(8,128)(2,1)S(1)} %bitcast.83), channel_id=1, replica_groups=mesh['dp'=8,'blk'=2,'ulysses'=8] {'ulysses'}, dimensions={1} | all-to-all | bytes 3145728 | tf_op jit(solution)/shard_map/all_to_all | solution.py:54
  61.0 1.7 copy.63
  63.4 5.4 %all-to-all-start.2 = ((bf16[32,8,384]{2,0,1:T(8,128)(2,1)}), bf16[32,8,384]{2,0,1:T(8,128)(2,1)S(1)}, u32[]{:S(2)}, u32[]{:S(2)}) async-start(bf16[32,8,384]{2,0,1:T(8,128)(2,1)} %bitcast.61), calls=%async_computation.2 | async-start | bytes 393216 | tf_op jit(solution)/shard_map/all_to_all | solution.py:50
  69.5 4.0 all-to-all-done.2
  73.5 5.4 %all-to-all-start.4 = ((bf16[32,8,384]{2,0,1:T(8,128)(2,1)}), bf16[32,8,384]{2,0,1:T(8,128)(2,1)S(1)}, u32[]{:S(2)}, u32[]{:S(2)}) async-start(bf16[32,8,384]{2,0,1:T(8,128)(2,1)} %bitcast.60), calls=%async_computation.4 | async-start | bytes 393216 | tf_op jit(solution)/shard_map/all_to_all | solution.py:51
  78.9 1.6 copy.98
  80.6 3.1 all-to-all-done.4
  83.7 5.4 %all-to-all-start.5 = ((bf16[32,8,384]{2,0,1:T(8,128)(2,1)}), bf16[32,8,384]{2,0,1:T(8,128)(2,1)S(1)}, u32[]{:S(2)}, u32[]{:S(2)}) async-start(bf16[32,8,384]{2,0,1:T(8,128)(2,1)} %bitcast.59), calls=%async_computation.5 | async-start | bytes 393216 | tf_op jit(solution)/shard_map/all_to_all | solution.py:52
  89.1 1.6 copy.57
  90.7 3.2 all-to-all-done.5
  94.5 6.3 %all-to-all-start.1 = ((bf16[256,8,384]{0,2,1:T(8,128)(2,1)}), bf16[256,8,384]{0,2,1:T(8,128)(2,1)}, u32[]{:S(2)}, u32[]{:S(2)}) async-start(bf16[256,8,384]{0,2,1:T(8,128)(2,1)} %bitcast.3), calls=%async_computation.1 | async-start | bytes 3145728 | tf_op jit(solution)/shard_map/all_to_all | solution.py:49
  101.5 1.7 concatenate.9
  103.2 1.6 copy.61
  104.8 1.7 reshape.55
  106.5 1.7 reshape.56
  108.2 12.2 %all-to-all-done.1 = bf16[256,8,384]{0,2,1:T(8,128)(2,1)} async-done(((bf16[256,8,384]{0,2,1:T(8,128)(2,1)}), bf16[256,8,384]{0,2,1:T(8,128)(2,1)}, u32[]{:S(2)}, u32[]{:S(2)}) %all-to-all-start.1) | async-done | bytes 1572896 | tf_op jit(solution)/shard_map/all_to_all | solution.py:49
  120.4 3.4 copy.58
  123.8 3.7 concatenate.8
  127.6 2.6 copy.60
  130.2 3.0 pad_maximum_fusion
  133.2 4.6 %fusion.19 = (f32[3,2304]{1,0:T(4,128)}, f32[3,2304,256]{1,2,0:T(8,128)}) fusion(pred[256]{0:T(512)(128)(4,1)S(1)} %iota_compare_fusion, bf16[256,3,128]{2,1,0:T(4,128)(2,1)S(1)} %copy-done.13, bf16[256,3,128]{2,0,1:T(8,128)(2,1)S(1)} %copy-done.8, bf16[2048,3,128]{2,0,1:T(8,128)(2,1)S(1)} %copy-done), kind=kOutput, calls=%fused_computation.24 | convolution fusion | flops 461825280 | bytes 9071872 | tf_op jit(solution)/shard_map/qhd,khd->hqk/dot_general | solution.py:15
  137.8 9.0 %reshape.57 = bf16[8,512,3,128]{3,2,1,0:T(4,128)(2,1)} reshape(bf16[4096,384]{1,0:T(8,128)(2,1)} %all-gather.3.cloned.1.call-done) | data formatting | bytes 6291456 | tf_op jit(solution)/shard_map/reshape;reshape | solution.py:32
  146.8 4.6 %copy.65 = bf16[8,512,3,128]{3,1,2,0:T(8,128)(2,1)} copy(bf16[8,512,3,128]{3,2,1,0:T(4,128)(2,1)} %reshape.57) | data formatting | bytes 6291456
  151.4 9.0 %reshape.58 = bf16[8,512,3,128]{3,2,1,0:T(4,128)(2,1)} reshape(bf16[4096,384]{1,0:T(8,128)(2,1)} %all-gather.5.cloned.1.call-done) | data formatting | bytes 6291456 | tf_op jit(solution)/shard_map/reshape;reshape | solution.py:33
  160.4 4.8 %copy.66 = bf16[8,512,3,128]{3,1,2,0:T(8,128)(2,1)} copy(bf16[8,512,3,128]{3,2,1,0:T(4,128)(2,1)} %reshape.58) | data formatting | bytes 6291456
  165.2 205.7 %while.15 = (s32[]{:T(128)}, f32[3,2304]{1,0:T(4,128)}, f32[3,2304]{1,0:T(4,128)}, f32[3,2304,128]{2,1,0:T(8,128)S(1)}, bf16[8,512,3,128]{3,1,2,0:T(8,128)(2,1)}...) while((s32[]{:T(128)}, f32[3,2304]{1,0:T(4,128)}, ...), condition=%wide.region_3.4_spmd.clone, body=%wide.region_0.3_spmd.clone.sunk | while | flops 1842939648 | bytes 52876476 | solution.py:39
  165.2 9.3 %bitcast_reduce_fusion.2 = (f32[3,2304]{1,0:T(4,128)}, f32[3,512,2304]{2,1,0:T(8,128)}) fusion(bf16[2304,3,128]{2,0,1:T(8,128)(2,1)} %get-tuple-element.187, bf16[8,512,3,128]{3,1,2,0:T(8,128)(2,1)} %get-tuple-element.186, s32[]{:T(128)} %get-tuple-element.173), kind=kOutput, calls=%fused_computation.1.clone.1 | convolution fusion | flops 913040640 | bytes 16346624 | tf_op jit(solution)/shard_map/while/body/eval_jaxpr/qhd,khd->hqk/dot_general | solution.py:15
  175.3 7.4 %fusion.47 = f32[3,2304]{1,0:T(4,128)S(1)} fusion(f32[3,512,2304]{2,1,0:T(8,128)} %get-tuple-element.161, f32[3,2304]{1,0:T(4,128)S(1)} %select_maximum_fusion.2), kind=kLoop, calls=%fused_computation.4.clone.1 | loop fusion | flops 10609920 | bytes 14211072 | tf_op jit(solution)/shard_map/while/body/eval_jaxpr/reduce_sum | solution.py:22
  182.7 7.5 %fusion.49 = f32[3,2304,128]{2,1,0:T(8,128)S(1)} fusion(f32[3,512,2304]{2,1,0:T(8,128)} %get-tuple-element.161, f32[3,2304]{1,0:T(4,128)S(1)} %select_maximum_fusion.2, f32[3,2304,128]{2,1,0:T(8,128)S(1)} %get-tuple-element.176, f32[3,2304]{1,0:T(4,128)S(1)} %get-tuple-element.163, pred[]{:T(512)S(6)} %compare.3, ...), kind=kOutput, calls=%fused_computation.8.clone.1 | convolution fusion | flops 919240704 | bytes 21682688 | tf_op jit(solution)/shard_map/while/body/eval_jaxpr/hqk,khd->hqd/dot_general | solution.py:23
  190.9 9.3 %bitcast_reduce_fusion.2 = (f32[3,2304]{1,0:T(4,128)}, f32[3,512,2304]{2,1,0:T(8,128)}) fusion(bf16[2304,3,128]{2,0,1:T(8,128)(2,1)} %get-tuple-element.187, bf16[8,512,3,128]{3,1,2,0:T(8,128)(2,1)} %get-tuple-element.186, s32[]{:T(128)} %get-tuple-element.173), kind=kOutput, calls=%fused_computation.1.clone.1 | convolution fusion | flops 913040640 | bytes 16346624 | tf_op jit(solution)/shard_map/while/body/eval_jaxpr/qhd,khd->hqk/dot_general | solution.py:15
  201.0 7.4 %fusion.47 = f32[3,2304]{1,0:T(4,128)S(1)} fusion(f32[3,512,2304]{2,1,0:T(8,128)} %get-tuple-element.161, f32[3,2304]{1,0:T(4,128)S(1)} %select_maximum_fusion.2), kind=kLoop, calls=%fused_computation.4.clone.1 | loop fusion | flops 10609920 | bytes 14211072 | tf_op jit(solution)/shard_map/while/body/eval_jaxpr/reduce_sum | solution.py:22
  208.5 7.5 %fusion.49 = f32[3,2304,128]{2,1,0:T(8,128)S(1)} fusion(f32[3,512,2304]{2,1,0:T(8,128)} %get-tuple-element.161, f32[3,2304]{1,0:T(4,128)S(1)} %select_maximum_fusion.2, f32[3,2304,128]{2,1,0:T(8,128)S(1)} %get-tuple-element.176, f32[3,2304]{1,0:T(4,128)S(1)} %get-tuple-element.163, pred[]{:T(512)S(6)} %compare.3, ...), kind=kOutput, calls=%fused_computation.8.clone.1 | convolution fusion | flops 919240704 | bytes 21682688 | tf_op jit(solution)/shard_map/while/body/eval_jaxpr/hqk,khd->hqd/dot_general | solution.py:23
  216.6 9.3 %bitcast_reduce_fusion.2 = (f32[3,2304]{1,0:T(4,128)}, f32[3,512,2304]{2,1,0:T(8,128)}) fusion(bf16[2304,3,128]{2,0,1:T(8,128)(2,1)} %get-tuple-element.187, bf16[8,512,3,128]{3,1,2,0:T(8,128)(2,1)} %get-tuple-element.186, s32[]{:T(128)} %get-tuple-element.173), kind=kOutput, calls=%fused_computation.1.clone.1 | convolution fusion | flops 913040640 | bytes 16346624 | tf_op jit(solution)/shard_map/while/body/eval_jaxpr/qhd,khd->hqk/dot_general | solution.py:15
  225.9 0.8 select_maximum_fusion.2
  226.7 7.4 %fusion.47 = f32[3,2304]{1,0:T(4,128)S(1)} fusion(f32[3,512,2304]{2,1,0:T(8,128)} %get-tuple-element.161, f32[3,2304]{1,0:T(4,128)S(1)} %select_maximum_fusion.2), kind=kLoop, calls=%fused_computation.4.clone.1 | loop fusion | flops 10609920 | bytes 14211072 | tf_op jit(solution)/shard_map/while/body/eval_jaxpr/reduce_sum | solution.py:22
  234.2 7.5 %fusion.49 = f32[3,2304,128]{2,1,0:T(8,128)S(1)} fusion(f32[3,512,2304]{2,1,0:T(8,128)} %get-tuple-element.161, f32[3,2304]{1,0:T(4,128)S(1)} %select_maximum_fusion.2, f32[3,2304,128]{2,1,0:T(8,128)S(1)} %get-tuple-element.176, f32[3,2304]{1,0:T(4,128)S(1)} %get-tuple-element.163, pred[]{:T(512)S(6)} %compare.3, ...), kind=kOutput, calls=%fused_computation.8.clone.1 | convolution fusion | flops 919240704 | bytes 21682688 | tf_op jit(solution)/shard_map/while/body/eval_jaxpr/hqk,khd->hqd/dot_general | solution.py:23
  242.3 9.3 %bitcast_reduce_fusion.2 = (f32[3,2304]{1,0:T(4,128)}, f32[3,512,2304]{2,1,0:T(8,128)}) fusion(bf16[2304,3,128]{2,0,1:T(8,128)(2,1)} %get-tuple-element.187, bf16[8,512,3,128]{3,1,2,0:T(8,128)(2,1)} %get-tuple-element.186, s32[]{:T(128)} %get-tuple-element.173), kind=kOutput, calls=%fused_computation.1.clone.1 | convolution fusion | flops 913040640 | bytes 16346624 | tf_op jit(solution)/shard_map/while/body/eval_jaxpr/qhd,khd->hqk/dot_general | solution.py:15
  252.4 7.4 %fusion.47 = f32[3,2304]{1,0:T(4,128)S(1)} fusion(f32[3,512,2304]{2,1,0:T(8,128)} %get-tuple-element.161, f32[3,2304]{1,0:T(4,128)S(1)} %select_maximum_fusion.2), kind=kLoop, calls=%fused_computation.4.clone.1 | loop fusion | flops 10609920 | bytes 14211072 | tf_op jit(solution)/shard_map/while/body/eval_jaxpr/reduce_sum | solution.py:22
  259.9 7.5 %fusion.49 = f32[3,2304,128]{2,1,0:T(8,128)S(1)} fusion(f32[3,512,2304]{2,1,0:T(8,128)} %get-tuple-element.161, f32[3,2304]{1,0:T(4,128)S(1)} %select_maximum_fusion.2, f32[3,2304,128]{2,1,0:T(8,128)S(1)} %get-tuple-element.176, f32[3,2304]{1,0:T(4,128)S(1)} %get-tuple-element.163, pred[]{:T(512)S(6)} %compare.3, ...), kind=kOutput, calls=%fused_computation.8.clone.1 | convolution fusion | flops 919240704 | bytes 21682688 | tf_op jit(solution)/shard_map/while/body/eval_jaxpr/hqk,khd->hqd/dot_general | solution.py:23
  268.0 9.3 %bitcast_reduce_fusion.2 = (f32[3,2304]{1,0:T(4,128)}, f32[3,512,2304]{2,1,0:T(8,128)}) fusion(bf16[2304,3,128]{2,0,1:T(8,128)(2,1)} %get-tuple-element.187, bf16[8,512,3,128]{3,1,2,0:T(8,128)(2,1)} %get-tuple-element.186, s32[]{:T(128)} %get-tuple-element.173), kind=kOutput, calls=%fused_computation.1.clone.1 | convolution fusion | flops 913040640 | bytes 16346624 | tf_op jit(solution)/shard_map/while/body/eval_jaxpr/qhd,khd->hqk/dot_general | solution.py:15
  278.1 7.4 %fusion.47 = f32[3,2304]{1,0:T(4,128)S(1)} fusion(f32[3,512,2304]{2,1,0:T(8,128)} %get-tuple-element.161, f32[3,2304]{1,0:T(4,128)S(1)} %select_maximum_fusion.2), kind=kLoop, calls=%fused_computation.4.clone.1 | loop fusion | flops 10609920 | bytes 14211072 | tf_op jit(solution)/shard_map/while/body/eval_jaxpr/reduce_sum | solution.py:22
  285.6 7.5 %fusion.49 = f32[3,2304,128]{2,1,0:T(8,128)S(1)} fusion(f32[3,512,2304]{2,1,0:T(8,128)} %get-tuple-element.161, f32[3,2304]{1,0:T(4,128)S(1)} %select_maximum_fusion.2, f32[3,2304,128]{2,1,0:T(8,128)S(1)} %get-tuple-element.176, f32[3,2304]{1,0:T(4,128)S(1)} %get-tuple-element.163, pred[]{:T(512)S(6)} %compare.3, ...), kind=kOutput, calls=%fused_computation.8.clone.1 | convolution fusion | flops 919240704 | bytes 21682688 | tf_op jit(solution)/shard_map/while/body/eval_jaxpr/hqk,khd->hqd/dot_general | solution.py:23
  293.8 9.3 %bitcast_reduce_fusion.2 = (f32[3,2304]{1,0:T(4,128)}, f32[3,512,2304]{2,1,0:T(8,128)}) fusion(bf16[2304,3,128]{2,0,1:T(8,128)(2,1)} %get-tuple-element.187, bf16[8,512,3,128]{3,1,2,0:T(8,128)(2,1)} %get-tuple-element.186, s32[]{:T(128)} %get-tuple-element.173), kind=kOutput, calls=%fused_computation.1.clone.1 | convolution fusion | flops 913040640 | bytes 16346624 | tf_op jit(solution)/shard_map/while/body/eval_jaxpr/qhd,khd->hqk/dot_general | solution.py:15
  303.9 7.4 %fusion.47 = f32[3,2304]{1,0:T(4,128)S(1)} fusion(f32[3,512,2304]{2,1,0:T(8,128)} %get-tuple-element.161, f32[3,2304]{1,0:T(4,128)S(1)} %select_maximum_fusion.2), kind=kLoop, calls=%fused_computation.4.clone.1 | loop fusion | flops 10609920 | bytes 14211072 | tf_op jit(solution)/shard_map/while/body/eval_jaxpr/reduce_sum | solution.py:22
  311.3 7.5 %fusion.49 = f32[3,2304,128]{2,1,0:T(8,128)S(1)} fusion(f32[3,512,2304]{2,1,0:T(8,128)} %get-tuple-element.161, f32[3,2304]{1,0:T(4,128)S(1)} %select_maximum_fusion.2, f32[3,2304,128]{2,1,0:T(8,128)S(1)} %get-tuple-element.176, f32[3,2304]{1,0:T(4,128)S(1)} %get-tuple-element.163, pred[]{:T(512)S(6)} %compare.3, ...), kind=kOutput, calls=%fused_computation.8.clone.1 | convolution fusion | flops 919240704 | bytes 21682688 | tf_op jit(solution)/shard_map/while/body/eval_jaxpr/hqk,khd->hqd/dot_general | solution.py:23
  319.5 9.3 %bitcast_reduce_fusion.2 = (f32[3,2304]{1,0:T(4,128)}, f32[3,512,2304]{2,1,0:T(8,128)}) fusion(bf16[2304,3,128]{2,0,1:T(8,128)(2,1)} %get-tuple-element.187, bf16[8,512,3,128]{3,1,2,0:T(8,128)(2,1)} %get-tuple-element.186, s32[]{:T(128)} %get-tuple-element.173), kind=kOutput, calls=%fused_computation.1.clone.1 | convolution fusion | flops 913040640 | bytes 16346624 | tf_op jit(solution)/shard_map/while/body/eval_jaxpr/qhd,khd->hqk/dot_general | solution.py:15
  329.6 7.4 %fusion.47 = f32[3,2304]{1,0:T(4,128)S(1)} fusion(f32[3,512,2304]{2,1,0:T(8,128)} %get-tuple-element.161, f32[3,2304]{1,0:T(4,128)S(1)} %select_maximum_fusion.2), kind=kLoop, calls=%fused_computation.4.clone.1 | loop fusion | flops 10609920 | bytes 14211072 | tf_op jit(solution)/shard_map/while/body/eval_jaxpr/reduce_sum | solution.py:22
  337.0 7.5 %fusion.49 = f32[3,2304,128]{2,1,0:T(8,128)S(1)} fusion(f32[3,512,2304]{2,1,0:T(8,128)} %get-tuple-element.161, f32[3,2304]{1,0:T(4,128)S(1)} %select_maximum_fusion.2, f32[3,2304,128]{2,1,0:T(8,128)S(1)} %get-tuple-element.176, f32[3,2304]{1,0:T(4,128)S(1)} %get-tuple-element.163, pred[]{:T(512)S(6)} %compare.3, ...), kind=kOutput, calls=%fused_computation.8.clone.1 | convolution fusion | flops 919240704 | bytes 21682688 | tf_op jit(solution)/shard_map/while/body/eval_jaxpr/hqk,khd->hqd/dot_general | solution.py:23
  345.2 9.3 %bitcast_reduce_fusion.2 = (f32[3,2304]{1,0:T(4,128)}, f32[3,512,2304]{2,1,0:T(8,128)}) fusion(bf16[2304,3,128]{2,0,1:T(8,128)(2,1)} %get-tuple-element.187, bf16[8,512,3,128]{3,1,2,0:T(8,128)(2,1)} %get-tuple-element.186, s32[]{:T(128)} %get-tuple-element.173), kind=kOutput, calls=%fused_computation.1.clone.1 | convolution fusion | flops 913040640 | bytes 16346624 | tf_op jit(solution)/shard_map/while/body/eval_jaxpr/qhd,khd->hqk/dot_general | solution.py:15
  355.3 7.4 %fusion.47 = f32[3,2304]{1,0:T(4,128)S(1)} fusion(f32[3,512,2304]{2,1,0:T(8,128)} %get-tuple-element.161, f32[3,2304]{1,0:T(4,128)S(1)} %select_maximum_fusion.2), kind=kLoop, calls=%fused_computation.4.clone.1 | loop fusion | flops 10609920 | bytes 14211072 | tf_op jit(solution)/shard_map/while/body/eval_jaxpr/reduce_sum | solution.py:22
  362.7 7.5 %fusion.49 = f32[3,2304,128]{2,1,0:T(8,128)S(1)} fusion(f32[3,512,2304]{2,1,0:T(8,128)} %get-tuple-element.161, f32[3,2304]{1,0:T(4,128)S(1)} %select_maximum_fusion.2, f32[3,2304,128]{2,1,0:T(8,128)S(1)} %get-tuple-element.176, f32[3,2304]{1,0:T(4,128)S(1)} %get-tuple-element.163, pred[]{:T(512)S(6)} %compare.3, ...), kind=kOutput, calls=%fused_computation.8.clone.1 | convolution fusion | flops 919240704 | bytes 21682688 | tf_op jit(solution)/shard_map/while/body/eval_jaxpr/hqk,khd->hqd/dot_general | solution.py:23
  370.9 3.0 copy.69
  374.7 5.0 %fusion.20 = f32[3,2304]{1,0:T(4,128)S(1)} fusion(f32[3,2304,256]{1,2,0:T(8,128)} %get-tuple-element.112, f32[3,2304]{1,0:T(4,128)S(1)} %max.6, pred[256]{0:T(512)(128)(4,1)S(1)} %iota_compare_fusion), kind=kLoop, calls=%fused_computation.25 | loop fusion | flops 8840448 | bytes 7133440 | tf_op jit(solution)/shard_map/reduce_sum | solution.py:22
  379.8 5.1 %fusion.24 = bf16[2304,3,128]{0,2,1:T(8,128)(2,1)S(1)} fusion(f32[3,2304,256]{1,2,0:T(8,128)} %get-tuple-element.112, f32[3,2304]{1,0:T(4,128)S(1)} %max.6, f32[3,2304,128]{1,2,0:T(8,128)S(1)} %copy-done.3, pred[256]{0:T(512)(128)(4,1)S(1)} %iota_compare_fusion, f32[3,2304]{1,0:T(4,128)S(1)} %get-tuple-element.107, f32[3,2304]{1,0:T(4,128)S(1)} %get-tuple-element.108, ...), kind=kOutput, calls=%fused_computation.30 | convolution fusion | flops 465371136 | bytes 12666112 | tf_op jit(solution)/shard_map/hqk,khd->hqd/dot_general | solution.py:23
  385.8 5.4 %all-to-all-start.7 = ((bf16[8,16,384]{2,1,0:T(8,128)(2,1)}), bf16[8,16,384]{2,1,0:T(8,128)(2,1)S(1)}, u32[]{:S(2)}, u32[]{:S(2)}) async-start(bf16[8,16,384]{2,1,0:T(8,128)(2,1)} %bitcast.16), calls=%async_computation.7 | async-start | bytes 196608 | tf_op jit(solution)/shard_map/all_to_all | solution.py:88
  391.9 1.5 copy.73
  393.3 1.5 all-to-all-done.7
  394.9 5.6 %all-to-all-start.6 = ((bf16[8,256,384]{1,2,0:T(8,128)(2,1)}), bf16[8,256,384]{1,2,0:T(8,128)(2,1)S(1)}, u32[]{:S(2)}, u32[]{:S(2)}) async-start(bf16[8,256,384]{1,2,0:T(8,128)(2,1)} %copy.73), calls=%async_computation.6 | async-start | bytes 3145728 | tf_op jit(solution)/shard_map/all_to_all | solution.py:87
  401.1 18.8 %all-to-all-done.6 = bf16[8,256,384]{1,2,0:T(8,128)(2,1)S(1)} async-done(((bf16[8,256,384]{1,2,0:T(8,128)(2,1)}), bf16[8,256,384]{1,2,0:T(8,128)(2,1)S(1)}, u32[]{:S(2)}, u32[]{:S(2)}) %all-to-all-start.6) | async-done | bytes 1572896 | tf_op jit(solution)/shard_map/all_to_all | solution.py:87
  419.9 1.7 copy.76
  (117 shorter events, 16.2 us)
Async XLA Ops:
  7.2 130.7 %all-gather.3.cloned.1.call-start = ((), (), s32[]{:S(2)}) async-start(), calls=%async_computation.8 | async-start | bytes 4718592 | tf_op jit(solution)/shard_map/all_gather | solution.py:71
  34.8 116.6 %all-gather.5.cloned.1.call-start = ((), (), s32[]{:S(2)}) async-start(), calls=%async_computation.9 | async-start | bytes 4718592 | tf_op jit(solution)/shard_map/all_gather | solution.py:72
  36.6 26.1 %copy-start.14 = (bf16[32,3072]{1,0:T(8,128)(2,1)S(1)}, bf16[32,3072]{1,0:T(8,128)(2,1)}, u32[]{:S(2)}) copy-start(bf16[32,3072]{1,0:T(8,128)(2,1)} %param.12) | copy-start | bytes 589828
  61.0 7.8 %copy-start.15 = (bf16[32,3072]{1,0:T(8,128)(2,1)S(1)}, bf16[32,3072]{1,0:T(8,128)(2,1)}, u32[]{:S(2)}) copy-start(bf16[32,3072]{1,0:T(8,128)(2,1)} %param.13) | copy-start | bytes 589828
  61.0 28.1 %copy-start.4 = (bf16[256,3072]{1,0:T(8,128)(2,1)S(1)}, bf16[256,3072]{1,0:T(8,128)(2,1)}, u32[]{:S(2)}) copy-start(bf16[256,3072]{1,0:T(8,128)(2,1)} %param.9) | copy-start | bytes 4718596
  63.4 10.1 %all-to-all-start.2 = ((bf16[32,8,384]{2,0,1:T(8,128)(2,1)}), bf16[32,8,384]{2,0,1:T(8,128)(2,1)S(1)}, u32[]{:S(2)}, u32[]{:S(2)}) async-start(bf16[32,8,384]{2,0,1:T(8,128)(2,1)} %bitcast.61), calls=%async_computation.2 | async-start | bytes 393216 | tf_op jit(solution)/shard_map/all_to_all | solution.py:50
  73.5 20.3 %copy-start.9 = (bf16[32,8,384]{2,0,1:T(8,128)(2,1)}, bf16[32,8,384]{2,0,1:T(8,128)(2,1)S(1)}, u32[]{:S(2)}) copy-start(bf16[32,8,384]{2,0,1:T(8,128)(2,1)S(1)} %all-to-all-done.2) | copy-start | bytes 589828
  73.5 10.2 %all-to-all-start.4 = ((bf16[32,8,384]{2,0,1:T(8,128)(2,1)}), bf16[32,8,384]{2,0,1:T(8,128)(2,1)S(1)}, u32[]{:S(2)}, u32[]{:S(2)}) async-start(bf16[32,8,384]{2,0,1:T(8,128)(2,1)} %bitcast.60), calls=%async_computation.4 | async-start | bytes 393216 | tf_op jit(solution)/shard_map/all_to_all | solution.py:51
  83.7 10.2 %copy-start.10 = (bf16[32,8,384]{2,0,1:T(8,128)(2,1)}, bf16[32,8,384]{2,0,1:T(8,128)(2,1)S(1)}, u32[]{:S(2)}) copy-start(bf16[32,8,384]{2,0,1:T(8,128)(2,1)S(1)} %all-to-all-done.4) | copy-start | bytes 589828
  83.7 10.2 %all-to-all-start.5 = ((bf16[32,8,384]{2,0,1:T(8,128)(2,1)}), bf16[32,8,384]{2,0,1:T(8,128)(2,1)S(1)}, u32[]{:S(2)}, u32[]{:S(2)}) async-start(bf16[32,8,384]{2,0,1:T(8,128)(2,1)} %bitcast.59), calls=%async_computation.5 | async-start | bytes 393216 | tf_op jit(solution)/shard_map/all_to_all | solution.py:52
  93.8 0.7 copy-start.11
  94.5 25.9 %all-to-all-start.1 = ((bf16[256,8,384]{0,2,1:T(8,128)(2,1)}), bf16[256,8,384]{0,2,1:T(8,128)(2,1)}, u32[]{:S(2)}, u32[]{:S(2)}) async-start(bf16[256,8,384]{0,2,1:T(8,128)(2,1)} %bitcast.3), calls=%async_computation.1 | async-start | bytes 3145728 | tf_op jit(solution)/shard_map/all_to_all | solution.py:49
  130.2 3.0 copy-start
  130.2 3.0 copy-start.8
  130.2 3.0 copy-start.13
  175.3 7.4 %copy-start.1 = (f32[3,2304]{1,0:T(4,128)S(1)}, f32[3,2304]{1,0:T(4,128)}, u32[]{:S(2)}) copy-start(f32[3,2304]{1,0:T(4,128)} %get-tuple-element.174) | copy-start | bytes 82948 | tf_op jit(solution)/shard_map/while
  175.3 7.4 %copy-start.5 = (f32[3,2304]{1,0:T(4,128)S(1)}, f32[3,2304]{1,0:T(4,128)}, u32[]{:S(2)}) copy-start(f32[3,2304]{1,0:T(4,128)} %get-tuple-element.175) | copy-start | bytes 82948 | tf_op jit(solution)/shard_map/while
  182.7 7.5 %copy-start.6 = (f32[3,2304]{1,0:T(4,128)}, f32[3,2304]{1,0:T(4,128)S(1)}, u32[]{:S(2)}) copy-start(f32[3,2304]{1,0:T(4,128)S(1)} %get-tuple-element.184) | copy-start | bytes 82948 | tf_op jit(solution)/shard_map/while
  201.0 7.4 %copy-start.1 = (f32[3,2304]{1,0:T(4,128)S(1)}, f32[3,2304]{1,0:T(4,128)}, u32[]{:S(2)}) copy-start(f32[3,2304]{1,0:T(4,128)} %get-tuple-element.174) | copy-start | bytes 82948 | tf_op jit(solution)/shard_map/while
  201.0 7.4 %copy-start.5 = (f32[3,2304]{1,0:T(4,128)S(1)}, f32[3,2304]{1,0:T(4,128)}, u32[]{:S(2)}) copy-start(f32[3,2304]{1,0:T(4,128)} %get-tuple-element.175) | copy-start | bytes 82948 | tf_op jit(solution)/shard_map/while
  208.5 7.5 %copy-start.6 = (f32[3,2304]{1,0:T(4,128)}, f32[3,2304]{1,0:T(4,128)S(1)}, u32[]{:S(2)}) copy-start(f32[3,2304]{1,0:T(4,128)S(1)} %get-tuple-element.184) | copy-start | bytes 82948 | tf_op jit(solution)/shard_map/while
  226.7 7.4 %copy-start.1 = (f32[3,2304]{1,0:T(4,128)S(1)}, f32[3,2304]{1,0:T(4,128)}, u32[]{:S(2)}) copy-start(f32[3,2304]{1,0:T(4,128)} %get-tuple-element.174) | copy-start | bytes 82948 | tf_op jit(solution)/shard_map/while
  226.7 7.4 %copy-start.5 = (f32[3,2304]{1,0:T(4,128)S(1)}, f32[3,2304]{1,0:T(4,128)}, u32[]{:S(2)}) copy-start(f32[3,2304]{1,0:T(4,128)} %get-tuple-element.175) | copy-start | bytes 82948 | tf_op jit(solution)/shard_map/while
  234.2 7.5 %copy-start.6 = (f32[3,2304]{1,0:T(4,128)}, f32[3,2304]{1,0:T(4,128)S(1)}, u32[]{:S(2)}) copy-start(f32[3,2304]{1,0:T(4,128)S(1)} %get-tuple-element.184) | copy-start | bytes 82948 | tf_op jit(solution)/shard_map/while
  252.4 7.4 %copy-start.1 = (f32[3,2304]{1,0:T(4,128)S(1)}, f32[3,2304]{1,0:T(4,128)}, u32[]{:S(2)}) copy-start(f32[3,2304]{1,0:T(4,128)} %get-tuple-element.174) | copy-start | bytes 82948 | tf_op jit(solution)/shard_map/while
  252.4 7.4 %copy-start.5 = (f32[3,2304]{1,0:T(4,128)S(1)}, f32[3,2304]{1,0:T(4,128)}, u32[]{:S(2)}) copy-start(f32[3,2304]{1,0:T(4,128)} %get-tuple-element.175) | copy-start | bytes 82948 | tf_op jit(solution)/shard_map/while
  259.9 7.5 %copy-start.6 = (f32[3,2304]{1,0:T(4,128)}, f32[3,2304]{1,0:T(4,128)S(1)}, u32[]{:S(2)}) copy-start(f32[3,2304]{1,0:T(4,128)S(1)} %get-tuple-element.184) | copy-start | bytes 82948 | tf_op jit(solution)/shard_map/while
  278.1 7.4 %copy-start.1 = (f32[3,2304]{1,0:T(4,128)S(1)}, f32[3,2304]{1,0:T(4,128)}, u32[]{:S(2)}) copy-start(f32[3,2304]{1,0:T(4,128)} %get-tuple-element.174) | copy-start | bytes 82948 | tf_op jit(solution)/shard_map/while
  278.1 7.4 %copy-start.5 = (f32[3,2304]{1,0:T(4,128)S(1)}, f32[3,2304]{1,0:T(4,128)}, u32[]{:S(2)}) copy-start(f32[3,2304]{1,0:T(4,128)} %get-tuple-element.175) | copy-start | bytes 82948 | tf_op jit(solution)/shard_map/while
  285.6 7.5 %copy-start.6 = (f32[3,2304]{1,0:T(4,128)}, f32[3,2304]{1,0:T(4,128)S(1)}, u32[]{:S(2)}) copy-start(f32[3,2304]{1,0:T(4,128)S(1)} %get-tuple-element.184) | copy-start | bytes 82948 | tf_op jit(solution)/shard_map/while
  303.8 7.4 %copy-start.1 = (f32[3,2304]{1,0:T(4,128)S(1)}, f32[3,2304]{1,0:T(4,128)}, u32[]{:S(2)}) copy-start(f32[3,2304]{1,0:T(4,128)} %get-tuple-element.174) | copy-start | bytes 82948 | tf_op jit(solution)/shard_map/while
  303.8 7.4 %copy-start.5 = (f32[3,2304]{1,0:T(4,128)S(1)}, f32[3,2304]{1,0:T(4,128)}, u32[]{:S(2)}) copy-start(f32[3,2304]{1,0:T(4,128)} %get-tuple-element.175) | copy-start | bytes 82948 | tf_op jit(solution)/shard_map/while
  311.3 7.5 %copy-start.6 = (f32[3,2304]{1,0:T(4,128)}, f32[3,2304]{1,0:T(4,128)S(1)}, u32[]{:S(2)}) copy-start(f32[3,2304]{1,0:T(4,128)S(1)} %get-tuple-element.184) | copy-start | bytes 82948 | tf_op jit(solution)/shard_map/while
  329.6 7.4 %copy-start.1 = (f32[3,2304]{1,0:T(4,128)S(1)}, f32[3,2304]{1,0:T(4,128)}, u32[]{:S(2)}) copy-start(f32[3,2304]{1,0:T(4,128)} %get-tuple-element.174) | copy-start | bytes 82948 | tf_op jit(solution)/shard_map/while
  329.6 7.4 %copy-start.5 = (f32[3,2304]{1,0:T(4,128)S(1)}, f32[3,2304]{1,0:T(4,128)}, u32[]{:S(2)}) copy-start(f32[3,2304]{1,0:T(4,128)} %get-tuple-element.175) | copy-start | bytes 82948 | tf_op jit(solution)/shard_map/while
  337.0 7.5 %copy-start.6 = (f32[3,2304]{1,0:T(4,128)}, f32[3,2304]{1,0:T(4,128)S(1)}, u32[]{:S(2)}) copy-start(f32[3,2304]{1,0:T(4,128)S(1)} %get-tuple-element.184) | copy-start | bytes 82948 | tf_op jit(solution)/shard_map/while
  355.3 7.4 %copy-start.1 = (f32[3,2304]{1,0:T(4,128)S(1)}, f32[3,2304]{1,0:T(4,128)}, u32[]{:S(2)}) copy-start(f32[3,2304]{1,0:T(4,128)} %get-tuple-element.174) | copy-start | bytes 82948 | tf_op jit(solution)/shard_map/while
  355.3 7.4 %copy-start.5 = (f32[3,2304]{1,0:T(4,128)S(1)}, f32[3,2304]{1,0:T(4,128)}, u32[]{:S(2)}) copy-start(f32[3,2304]{1,0:T(4,128)} %get-tuple-element.175) | copy-start | bytes 82948 | tf_op jit(solution)/shard_map/while
  362.7 7.5 %copy-start.6 = (f32[3,2304]{1,0:T(4,128)}, f32[3,2304]{1,0:T(4,128)S(1)}, u32[]{:S(2)}) copy-start(f32[3,2304]{1,0:T(4,128)S(1)} %get-tuple-element.184) | copy-start | bytes 82948 | tf_op jit(solution)/shard_map/while
  374.7 5.1 %copy-start.2 = (f32[3,2304]{1,0:T(4,128)S(1)}, f32[3,2304]{1,0:T(4,128)}, u32[]{:S(2)}) copy-start(f32[3,2304]{1,0:T(4,128)} %get-tuple-element.42) | copy-start | bytes 82948
  374.7 5.1 %copy-start.7 = (f32[3,2304]{1,0:T(4,128)S(1)}, f32[3,2304]{1,0:T(4,128)}, u32[]{:S(2)}) copy-start(f32[3,2304]{1,0:T(4,128)} %get-tuple-element.43) | copy-start | bytes 82948
  374.7 5.1 %copy-start.3 = (f32[3,2304,128]{1,2,0:T(8,128)S(1)}, f32[3,2304,128]{1,2,0:T(8,128)}, u32[]{:S(2)}) copy-start(f32[3,2304,128]{1,2,0:T(8,128)} %copy.69) | copy-start | bytes 10616836
  374.7 5.1 %copy-start.12 = (bf16[256,3,128]{2,1,0:T(4,128)(2,1)S(1)}, bf16[256,3,128]{2,1,0:T(4,128)(2,1)}, u32[]{:S(2)}) copy-start(bf16[256,3,128]{2,1,0:T(4,128)(2,1)} %reshape.56) | copy-start | bytes 589828
  385.8 9.1 %all-to-all-start.7 = ((bf16[8,16,384]{2,1,0:T(8,128)(2,1)}), bf16[8,16,384]{2,1,0:T(8,128)(2,1)S(1)}, u32[]{:S(2)}, u32[]{:S(2)}) async-start(bf16[8,16,384]{2,1,0:T(8,128)(2,1)} %bitcast.16), calls=%async_computation.7 | async-start | bytes 196608 | tf_op jit(solution)/shard_map/all_to_all | solution.py:88
  394.9 25.1 %all-to-all-start.6 = ((bf16[8,256,384]{1,2,0:T(8,128)(2,1)}), bf16[8,256,384]{1,2,0:T(8,128)(2,1)S(1)}, u32[]{:S(2)}, u32[]{:S(2)}) async-start(bf16[8,256,384]{1,2,0:T(8,128)(2,1)} %copy.73), calls=%async_computation.6 | async-start | bytes 3145728 | tf_op jit(solution)/shard_map/all_to_all | solution.py:87
Sparse Core Ops, SparseCore 0:
  35.0 49.3 all-gather.2
  86.0 48.4 all-gather.4
where the time goes:
time: 434 us; the launch traced here: 429 us
  matrix products  144 us (33%)
  other arithmetic  74.7 us (17%)
  local copies, waits for them, and re-layouts  69.1 us (16%)
  blocking collectives  48.7 us (11%)
  waiting for transfers between devices  42.9 us (10%)
  starting transfers between devices  33.6 us (8%)
  between operations  14.9 us (3%)
    dot_general x9, matrix products, attend_block(): jnp.einsum('qhd,khd->hqk', queries, keys, preferred_element_type=jnp.floa...  78.9 us
    dot_general x9, matrix products, attend_block(): jnp.einsum('hqk,khd->hqd', weights.astype(jnp.bfloat16), values, preferre...  65.3 us
    reduce_sum x9, other arithmetic, attend_block(): total = total * factor + jnp.sum(weights, axis=-1)  64 us
    all_to_all x1, blocking collectives, on_device(): lax.all_to_all(video_value, 'ulysses', split_axis=1, concat_axis=0, tiled...  24.4 us
    all_to_all x1, blocking collectives, on_device(): lax.all_to_all(video_key, 'ulysses', split_axis=1, concat_axis=0, tiled=T...  24.3 us
    all_to_all x1, waiting for transfers between devices, on_device(): lax.all_to_all(attended[:video_rows], 'ulysses', split_axis=0, concat_axi...  18.8 us
    unnamed x34, local copies, waits for them, and re-layouts  18.1 us
    all_to_all x1, waiting for transfers between devices, on_device(): lax.all_to_all(video_query, 'ulysses', split_axis=1, concat_axis=0, tiled...  12.2 us
  transfers between devices with their start and end apart: 8, of which 6 were waited for; matrix products, arithmetic and copies ran while one was open for 11% of the time, Pallas kernels for 0%

commit v1 on v0

v1 whole, which is shorter than its diff:
```python
import math

import jax
import jax.numpy as jnp
from jax import lax
from jax.experimental import pallas as pl
from jax.experimental.pallas import tpu as pltpu
from jax.sharding import PartitionSpec as P

MESH = pl.DeviceIdType.MESH
HEAD = 128
NEG_BIG = -1e30
SCALE = HEAD ** -0.5 * math.log2(math.e)
XS, ZS, CORES = 4, 2, 2
CHIPS = XS * ZS
HEADS_HERE = 3
ROWS = 256
TEXT_ROWS = 32
OUT_TEXT = 16
HALF = CHIPS * ROWS + XS * TEXT_ROWS
KEYS = CORES * HALF
PAIR = ZS * ROWS + TEXT_ROWS
PEERS = ((1, 0), (3, 0), (2, 0), (0, 1), (1, 1), (3, 1), (2, 1))
VIDEO_1 = CHIPS * ROWS + CORES * XS * TEXT_ROWS
BLOCKS = (
    (CHIPS * ROWS, VIDEO_1),
    (0, 1024),
    (1024, 2048),
    (VIDEO_1, VIDEO_1 + 1024),
    (VIDEO_1 + 1024, VIDEO_1 + 2048),
)


def dot(a, b, dims):
    return lax.dot_general(a, b, (dims, ((), ())), preferred_element_type=jnp.float32)


def wait_for(ref, sem):
    pltpu.make_async_copy(ref, ref, sem).wait()


def kernel(
    length, vq, vk, vv, tq, tk, tv, vo, to,
    keys, values, queries, outs,
    recv, send, sib_recv, sib_send, out_recv, out_send, text_recv, text_send,
):
    u = lax.axis_index("ulysses")
    z = lax.axis_index("blk")
    x, c = u // CORES, lax.rem(u, CORES)
    me = z * (XS * CORES) + u

    def device(px, pz, pc):
        return {"blk": pz, "ulysses": px * CORES + pc}

    barrier = pltpu.get_barrier_semaphore()
    for step in range(1, CHIPS * CORES):
        other = lax.rem(me + step, CHIPS * CORES)
        pl.semaphore_signal(
            barrier,
            inc=1,
            device_id={"blk": other // (XS * CORES), "ulysses": lax.rem(other, XS * CORES)},
            device_id_type=MESH,
        )
    pl.semaphore_wait(barrier, CHIPS * CORES - 1)

    def columns(px, pz, h):
        return pl.ds(pl.multiple_of(((px * ZS + pz) * HEADS_HERE + h) * HEAD, HEAD), HEAD)

    chip = x * ZS + z
    key_rows = pl.ds(pl.multiple_of(c * VIDEO_1 + chip * ROWS, 16), ROWS)
    key_text = pl.ds(
        pl.multiple_of(CHIPS * ROWS + c * (XS * TEXT_ROWS) + x * TEXT_ROWS, 16), TEXT_ROWS
    )
    query_rows = pl.ds(pl.multiple_of(x * PAIR + z * ROWS, 16), ROWS)
    query_text = pl.ds(pl.multiple_of(x * PAIR + ZS * ROWS, 16), TEXT_ROWS)
    mine = pl.ds(pl.multiple_of(c * HALF, 16), HALF)
    theirs = pl.ds(pl.multiple_of((1 - c) * HALF, 16), HALF)
    lanes = pl.ds(0, HEAD)

    def scatter(h, carry):
        for i, (video, text, place, rows, text_rows) in enumerate(
            (
                (vk, tk, keys, key_rows, key_text),
                (vv, tv, values, key_rows, key_text),
                (vq, tq, queries, query_rows, query_text),
            )
        ):
            land = place.at[h, rows, lanes]
            land_text = place.at[h, text_rows, lanes]
            for dx, dz in PEERS:
                px, pz = lax.rem(x + dx, XS), lax.rem(z + dz, ZS)
                pltpu.make_async_remote_copy(
                    src_ref=video.at[:, columns(px, pz, h)],
                    dst_ref=land,
                    send_sem=send.at[i, h],
                    recv_sem=recv.at[i, h],
                    device_id=device(px, pz, c),
                    device_id_type=MESH,
                ).start()
                if dz == 0:
                    pltpu.make_async_remote_copy(
                        src_ref=text.at[:, columns(px, pz, h)],
                        dst_ref=land_text,
                        send_sem=send.at[i, h],
                        recv_sem=recv.at[i, h],
                        device_id=device(px, pz, c),
                        device_id_type=MESH,
                    ).start()
            pltpu.make_async_copy(video.at[:, columns(x, z, h)], land, recv.at[i, h]).start()
            pltpu.make_async_copy(text.at[:, columns(x, z, h)], land_text, recv.at[i, h]).start()
        return carry

    lax.fori_loop(0, HEADS_HERE, scatter, 0)

    for h in range(HEADS_HERE):
        values[h, :, HEAD:] = jnp.ones((KEYS, HEAD), jnp.bfloat16)

    def to_sibling(i, place, h):
        wait_for(place.at[h, mine, lanes], recv.at[i, h])
        pltpu.make_async_remote_copy(
            src_ref=place.at[h, mine, lanes],
            dst_ref=place.at[h, mine, lanes],
            send_sem=sib_send.at[i, h],
            recv_sem=sib_recv.at[i, h],
            device_id=device(x, z, 1 - c),
            device_id_type=MESH,
        ).start()

    def attend(h, b):
        rows = pl.ds(pl.multiple_of(b * PAIR, 16), PAIR)
        q = queries[h, rows, :]
        t = lax.broadcasted_iota(jnp.int32, (1, CORES * XS * TEXT_ROWS), 1)
        part = XS * TEXT_ROWS
        position = (
            (lax.rem(t, part) // TEXT_ROWS) * (CORES * TEXT_ROWS)
            + (t // part) * TEXT_ROWS
            + lax.rem(t, TEXT_ROWS)
        )
        valid = position < length[0]
        top = None
        first, last = BLOCKS[0]
        scores = dot(q, keys[h, first:last, :], ((1,), (1,)))
        scores = jnp.where(valid, scores, NEG_BIG)
        for j, (first, last) in enumerate(BLOCKS):
            if j + 1 < len(BLOCKS):
                lo, hi = BLOCKS[j + 1]
                following = dot(q, keys[h, lo:hi, :], ((1,), (1,)))
            here = jnp.max(scores, axis=1, keepdims=True)
            new_top = here if top is None else jnp.maximum(top, here)
            weights = jnp.exp2(scores * SCALE - new_top * SCALE).astype(jnp.bfloat16)
            product = dot(weights, values[h, first:last, :], ((1,), (0,)))
            if top is None:
                summed = product
            else:
                summed = summed * jnp.exp2((top - new_top) * SCALE) + product
            top = new_top
            if j + 1 < len(BLOCKS):
                scores = following
        outs[h, rows, :] = (summed[:, :HEAD] / summed[:, HEAD:]).astype(jnp.bfloat16)

    def video_back(h, b, pz):
        return pltpu.make_async_remote_copy(
            src_ref=outs.at[h, pl.ds(pl.multiple_of(b * PAIR + pz * ROWS, 16), ROWS), :],
            dst_ref=vo.at[:, columns(x, z, h)],
            send_sem=out_send.at[h],
            recv_sem=out_recv,
            device_id=device(b, pz, c),
            device_id_type=MESH,
        )

    def text_place(h, b, k):
        src = outs.at[
            h, pl.ds(pl.multiple_of(b * PAIR + ZS * ROWS + k * OUT_TEXT, 16), OUT_TEXT), :
        ]
        px, pz = lax.rem(b * CORES + c, XS), (b * CORES + c) // XS
        own = (px == x) & (pz == z) & (c == k)
        return src, to.at[:, columns(x, z, h)], px, pz, own

    def text_back(h, b, k):
        src, dst, px, pz, own = text_place(h, b, k)
        return own, pltpu.make_async_remote_copy(
            src_ref=src,
            dst_ref=dst,
            send_sem=text_send.at[h],
            recv_sem=text_recv,
            device_id=device(px, pz, k),
            device_id_type=MESH,
        )

    to_sibling(0, keys, 0)
    to_sibling(1, values, 0)

    def turn(t, carry):
        h, i = t // XS, lax.rem(t, XS)
        b = lax.rem(x + 1 + i, XS)

        @pl.when(i == 0)
        def _():
            wait_for(queries.at[h], recv.at[2, h])
            wait_for(keys.at[h, theirs, lanes], sib_recv.at[0, h])
            wait_for(values.at[h, theirs, lanes], sib_recv.at[1, h])

        @pl.when((i == XS - 1) & (h < HEADS_HERE - 1))
        def _():
            to_sibling(0, keys, h + 1)

        attend(h, b)

        for dz in (1, 0):
            pz = lax.rem(z + dz, ZS)
            if dz == 1:
                video_back(h, b, pz).start()
            else:

                @pl.when(i < XS - 1)
                def _():
                    video_back(h, b, pz).start()

                @pl.when(i == XS - 1)
                def _():
                    pltpu.make_async_copy(
                        outs.at[h, query_rows, :], vo.at[:, columns(x, z, h)], out_recv
                    ).start()

        for k in range(CORES):
            own, copy = text_back(h, b, k)
            src, dst, _, _, _ = text_place(h, b, k)

            @pl.when(own)
            def _():
                pltpu.make_async_copy(src, dst, text_recv).start()

            @pl.when(jnp.logical_not(own))
            def _():
                copy.start()

        @pl.when((i == XS - 1) & (h < HEADS_HERE - 1))
        def _():
            to_sibling(1, values, h + 1)

        return carry

    lax.fori_loop(0, HEADS_HERE * XS, turn, 0)

    def finish(h, carry):
        for i in range(3):
            sent = (CHIPS - 1) * ROWS + (XS - 1) * TEXT_ROWS
            wait_for(outs.at[h, pl.ds(0, sent), :], send.at[i, h])
        for i, place in ((0, keys), (1, values)):
            wait_for(place.at[h, mine, lanes], sib_send.at[i, h])
        wait_for(outs.at[h, pl.ds(0, (CHIPS - 1) * ROWS), :], out_send.at[h])
        for b in range(XS):
            for k in range(CORES):
                own, copy = text_back(h, b, k)

                @pl.when(jnp.logical_not(own))
                def _():
                    copy.wait_send()

        return carry

    lax.fori_loop(0, HEADS_HERE, finish, 0)
    wait_for(vo, out_recv)
    wait_for(to, text_recv)


def on_device(video_query, video_key, video_value, text_query, text_key, text_value, text_length):
    any_spec = pl.BlockSpec(memory_space=pl.ANY)
    dma = pltpu.SemaphoreType.DMA
    width = video_query.shape[1]
    flops = 4 * HEADS_HERE * XS * PAIR * KEYS * HEAD
    return pl.pallas_call(
        kernel,
        out_shape=(
            jax.ShapeDtypeStruct((ROWS, width), jnp.bfloat16),
            jax.ShapeDtypeStruct((OUT_TEXT, width), jnp.bfloat16),
        ),
        in_specs=[pl.BlockSpec(memory_space=pltpu.SMEM)] + [any_spec] * 6,
        out_specs=(any_spec, any_spec),
        scratch_shapes=[
            pltpu.VMEM((HEADS_HERE, KEYS, HEAD), jnp.bfloat16),
            pltpu.VMEM((HEADS_HERE, KEYS, 2 * HEAD), jnp.bfloat16),
            pltpu.VMEM((HEADS_HERE, XS * PAIR, HEAD), jnp.bfloat16),
            pltpu.VMEM((HEADS_HERE, XS * PAIR, HEAD), jnp.bfloat16),
            dma((3, HEADS_HERE)),
            dma((3, HEADS_HERE)),
            dma((2, HEADS_HERE)),
            dma((2, HEADS_HERE)),
            dma,
            dma((HEADS_HERE,)),
            dma,
            dma((HEADS_HERE,)),
        ],
        cost_estimate=pl.CostEstimate(
            flops=flops, bytes_accessed=8 * ROWS * width, transcendentals=flops // (4 * HEAD)
        ),
        compiler_params=pltpu.CompilerParams(
            collective_id=0, has_side_effects=True, vmem_limit_bytes=52 * 2**20
        ),
        name="joint_attention",
    )(text_length, video_query, video_key, video_value, text_query, text_key, text_value)


def solution(mesh):
    assert mesh.shape["blk"] == ZS and mesh.shape["ulysses"] == XS * CORES
    tokens = P(("dp", "blk", "ulysses"), None)
    text = P(("dp", "ulysses"), None)
    return jax.shard_map(
        on_device,
        mesh=mesh,
        in_specs=(tokens, tokens, tokens, text, text, text, P("dp")),
        out_specs=(tokens, tokens),
        check_vma=False,
    )
```

time: 434 us -> 88.4 us (0.20); the launches traced: 429 us -> 88.1 us
  matrix products: 144 us -> 0 us
  Pallas kernels: 0 us -> 80.8 us
  other arithmetic: 74.7 us -> 0 us
  local copies, waits for them, and re-layouts: 69.1 us -> 6.06 us
  blocking collectives: 48.7 us -> 0 us
  waiting for transfers between devices: 42.9 us -> 0 us
  starting transfers between devices: 33.6 us -> 0 us
  between operations: 14.9 us -> 1.3 us
    dot_general x18 -> x0, matrix products: 144 us -> none  [the longest x9 78.9 us: attend_block(): jnp.einsum('qhd,khd->hqk', queries, keys, preferred_element_type=jnp.floa...]
    pallas_call x0 -> x1, Pallas kernels: none -> 80.8 us  [on_device(): pl.pallas_call(kernel, out_shape=(jax.ShapeDtypeStruct((ROWS, width), jnp...]
    reduce_sum x9 -> x0, other arithmetic: 64 us -> none  [attend_block(): total = total * factor + jnp.sum(weights, axis=-1)]
    all_to_all x2 -> x0, blocking collectives: 48.7 us -> none  [the longest x1 24.4 us: on_device(): lax.all_to_all(video_value, 'ulysses', split_axis=1, concat_axis=0, tiled...]
    all_to_all x6 -> x0, waiting for transfers between devices: 42.9 us -> none  [the longest x1 18.8 us: on_device(): lax.all_to_all(attended[:video_rows], 'ulysses', split_axis=0, concat_axi...]
    all_to_all x6 -> x0, starting transfers between devices: 33.5 us -> none  [the longest x1 6.31 us: on_device(): lax.all_to_all(video_query, 'ulysses', split_axis=1, concat_axis=0, tiled...]
    another operation x2 -> x0, local copies, waits for them, and re-layouts: 18 us -> none  [the longest x1 8.99 us: attend_video(): blocks_k = keys.reshape(count // width, width, keys.shape[1], keys.shape[2])]
    unnamed x34 -> x8, local copies, waits for them, and re-layouts: 18.1 us -> 6.06 us
  transfers between devices with their start and end apart: 8 -> 0, of which waited for: 6 -> 0; matrix products, arithmetic and copies ran while one was open for 11% -> 0% of each run, Pallas kernels for 0% -> 0%
where the time goes in v1:
time: 88.4 us; the launch traced here: 88.1 us
  Pallas kernels  80.8 us (91%)
  local copies, waits for them, and re-layouts  6.06 us (7%)
  between operations  1.3 us (1%)
    pallas_call x1, Pallas kernels, on_device(): pl.pallas_call(kernel, out_shape=(jax.ShapeDtypeStruct((ROWS, width), jnp...  80.8 us
    unnamed x8, local copies, waits for them, and re-layouts  6.06 us

profile of v1, /device:TPU:22, one launch (start us, length us, event | category | flops | bytes accessed | tf_op | source)
XLA Modules:
  0.0 88.1 jit_solution(12524662583541272795)
XLA Ops:
  1.3 0.0 copy-start
  1.3 0.9 %copy-done = bf16[32,3072]{1,0:T(8,128)(2,1)S(1)} copy-done((bf16[32,3072]{1,0:T(8,128)(2,1)S(1)}, bf16[32,3072]{1,0:T(8,128)(2,1)}, u32[]{:S(2)}) %copy-start) | copy-done | bytes 196632
  2.2 0.0 copy-start.1
  2.2 0.9 %copy-done.1 = bf16[32,3072]{1,0:T(8,128)(2,1)S(1)} copy-done((bf16[32,3072]{1,0:T(8,128)(2,1)S(1)}, bf16[32,3072]{1,0:T(8,128)(2,1)}, u32[]{:S(2)}) %copy-start.1) | copy-done | bytes 196632
  3.1 0.0 copy-start.2
  3.1 0.9 %copy-done.2 = bf16[32,3072]{1,0:T(8,128)(2,1)S(1)} copy-done((bf16[32,3072]{1,0:T(8,128)(2,1)S(1)}, bf16[32,3072]{1,0:T(8,128)(2,1)}, u32[]{:S(2)}) %copy-start.2) | copy-done | bytes 196632
  4.1 80.8 %joint_attention.1 = (bf16[256,3072]{1,0:T(8,128)(2,1)}, bf16[16,3072]{1,0:T(8,128)(2,1)S(1)}) custom-call(s32[1]{0:T(128)S(6)} %copy.11.length, bf16[256,3072]{1,0:T(8,128)(2,1)} %vq.1, bf16[256,3072]{1,0:T(8,128)(2,1)} %vk.1, bf16[256,3072]{1,0:T(8,128)(2,1)} %vv.1, bf16[32,3072]{1,0:T(8,128)(2,1)S(1)} %copy-done, bf16[32,3072]{1,0:T(8,128)(2,1)S(1)} %copy-done.1, ...), custom_call_target="tpu_custom_call" | custom-call | flops 14545846272 | bytes 6291456 | tf_op jit(solution)/shard_map/joint_attention/pallas_call | solution.py:272
  84.8 2.7 %copy.12 = bf16[256,3072]{1,0:T(8,128)(2,1)} copy(bf16[256,3072]{1,0:T(8,128)(2,1)} %get-tuple-element.4) | data formatting | bytes 3145728
  87.5 0.6 copy.13
Async XLA Ops:
  1.3 0.9 %copy-start = (bf16[32,3072]{1,0:T(8,128)(2,1)S(1)}, bf16[32,3072]{1,0:T(8,128)(2,1)}, u32[]{:S(2)}) copy-start(bf16[32,3072]{1,0:T(8,128)(2,1)} %tq.1) | copy-start | bytes 589828
  2.2 0.9 %copy-start.1 = (bf16[32,3072]{1,0:T(8,128)(2,1)S(1)}, bf16[32,3072]{1,0:T(8,128)(2,1)}, u32[]{:S(2)}) copy-start(bf16[32,3072]{1,0:T(8,128)(2,1)} %tk.1) | copy-start | bytes 589828
  3.1 0.9 %copy-start.2 = (bf16[32,3072]{1,0:T(8,128)(2,1)S(1)}, bf16[32,3072]{1,0:T(8,128)(2,1)}, u32[]{:S(2)}) copy-start(bf16[32,3072]{1,0:T(8,128)(2,1)} %tv.1) | copy-start | bytes 589828

commit v2 on v1

--- a/solution.py
+++ b/solution.py
@@ -21,6 +21,7 @@
 KEYS = CORES * HALF
 PAIR = ZS * ROWS + TEXT_ROWS
 PEERS = ((1, 0), (3, 0), (2, 0), (0, 1), (1, 1), (3, 1), (2, 1))
+QUERY_PEERS = ((3, 0), (3, 1), (2, 0), (2, 1), (1, 0), (1, 1), (0, 1))
 VIDEO_1 = CHIPS * ROWS + CORES * XS * TEXT_ROWS
 BLOCKS = (
     (CHIPS * ROWS, VIDEO_1),
@@ -40,28 +41,30 @@
 
 
 def kernel(
-    length, vq, vk, vv, tq, tk, tv, vo, to,
-    keys, values, queries, outs,
-    recv, send, sib_recv, sib_send, out_recv, out_send, text_recv, text_send,
+    length_in, vq, vk, vv, tq, tk, tv, vo, to,
+    keys, values, queries, outs, staged, length, length_sem, stage_send, stage_recv,
+    recv, query_recv, send, sib_recv, sib_send, out_recv, out_send, text_recv, text_send,
 ):
     u = lax.axis_index("ulysses")
     z = lax.axis_index("blk")
     x, c = u // CORES, lax.rem(u, CORES)
-    me = z * (XS * CORES) + u
 
     def device(px, pz, pc):
         return {"blk": pz, "ulysses": px * CORES + pc}
 
+    length_copy = pltpu.make_async_copy(length_in, length, length_sem)
+    length_copy.start()
+
     barrier = pltpu.get_barrier_semaphore()
-    for step in range(1, CHIPS * CORES):
-        other = lax.rem(me + step, CHIPS * CORES)
+    for dx, dz in PEERS:
         pl.semaphore_signal(
             barrier,
             inc=1,
-            device_id={"blk": other // (XS * CORES), "ulysses": lax.rem(other, XS * CORES)},
+            device_id=device(lax.rem(x + dx, XS), lax.rem(z + dz, ZS), c),
             device_id_type=MESH,
         )
-    pl.semaphore_wait(barrier, CHIPS * CORES - 1)
+    pl.semaphore_signal(barrier, inc=1, device_id=device(x, z, 1 - c), device_id_type=MESH)
+    pl.semaphore_wait(barrier, CHIPS)
 
     def columns(px, pz, h):
         return pl.ds(pl.multiple_of(((px * ZS + pz) * HEADS_HERE + h) * HEAD, HEAD), HEAD)
@@ -72,45 +75,55 @@
         pl.multiple_of(CHIPS * ROWS + c * (XS * TEXT_ROWS) + x * TEXT_ROWS, 16), TEXT_ROWS
     )
     query_rows = pl.ds(pl.multiple_of(x * PAIR + z * ROWS, 16), ROWS)
-    query_text = pl.ds(pl.multiple_of(x * PAIR + ZS * ROWS, 16), TEXT_ROWS)
+    own_text = pl.ds(pl.multiple_of(x * PAIR + ZS * ROWS + c * OUT_TEXT, 16), OUT_TEXT)
+    other_text = pl.ds(pl.multiple_of(x * PAIR + ZS * ROWS + (1 - c) * OUT_TEXT, 16), OUT_TEXT)
     mine = pl.ds(pl.multiple_of(c * HALF, 16), HALF)
     theirs = pl.ds(pl.multiple_of((1 - c) * HALF, 16), HALF)
     lanes = pl.ds(0, HEAD)
 
-    def scatter(h, carry):
-        for i, (video, text, place, rows, text_rows) in enumerate(
-            (
-                (vk, tk, keys, key_rows, key_text),
-                (vv, tv, values, key_rows, key_text),
-                (vq, tq, queries, query_rows, query_text),
-            )
-        ):
-            land = place.at[h, rows, lanes]
-            land_text = place.at[h, text_rows, lanes]
-            for dx, dz in PEERS:
-                px, pz = lax.rem(x + dx, XS), lax.rem(z + dz, ZS)
-                pltpu.make_async_remote_copy(
-                    src_ref=video.at[:, columns(px, pz, h)],
-                    dst_ref=land,
-                    send_sem=send.at[i, h],
-                    recv_sem=recv.at[i, h],
-                    device_id=device(px, pz, c),
-                    device_id_type=MESH,
-                ).start()
-                if dz == 0:
-                    pltpu.make_async_remote_copy(
-                        src_ref=text.at[:, columns(px, pz, h)],
-                        dst_ref=land_text,
-                        send_sem=send.at[i, h],
-                        recv_sem=recv.at[i, h],
-                        device_id=device(px, pz, c),
-                        device_id_type=MESH,
-                    ).start()
-            pltpu.make_async_copy(video.at[:, columns(x, z, h)], land, recv.at[i, h]).start()
-            pltpu.make_async_copy(text.at[:, columns(x, z, h)], land_text, recv.at[i, h]).start()
+    stage = pltpu.make_async_remote_copy(
+        src_ref=tq.at[pl.ds(pl.multiple_of((1 - c) * OUT_TEXT, 16), OUT_TEXT), :],
+        dst_ref=staged,
+        send_sem=stage_send,
+        recv_sem=stage_recv,
+        device_id=device(x, z, 1 - c),
+        device_id_type=MESH,
+    )
+    stage.start()
+
+    def scatter(h, pieces, dst, sems, peers):
+        for dx, dz in peers:
+            px, pz = lax.rem(x + dx, XS), lax.rem(z + dz, ZS)
+            pltpu.make_async_remote_copy(
+                src_ref=pieces.at[:, columns(px, pz, h)],
+                dst_ref=dst,
+                send_sem=sems[0],
+                recv_sem=sems[1],
+                device_id=device(px, pz, c),
+                device_id_type=MESH,
+            ).start()
+        pltpu.make_async_copy(pieces.at[:, columns(x, z, h)], dst, sems[1]).start()
+
+    text_peers = tuple(p for p in PEERS if p[1] == 0)
+    tq_own = tq.at[pl.ds(pl.multiple_of(c * OUT_TEXT, 16), OUT_TEXT), :]
+
+    def scatter_head(h, carry):
+        for i, (video, text, place) in enumerate(((vk, tk, keys), (vv, tv, values))):
+            sems = send.at[i, h], recv.at[i, h]
+            scatter(h, video, place.at[h, key_rows, lanes], sems, PEERS)
+            scatter(h, text, place.at[h, key_text, lanes], sems, text_peers)
+        sems = send.at[2, h], query_recv.at[h, x]
+        scatter(h, vq, queries.at[h, query_rows, :], sems, QUERY_PEERS)
+
+        @pl.when(h == 0)
+        def _():
+            stage.wait()
+
+        scatter(h, tq_own, queries.at[h, own_text, :], sems, text_peers)
+        scatter(h, staged, queries.at[h, other_text, :], sems, text_peers)
         return carry
 
-    lax.fori_loop(0, HEADS_HERE, scatter, 0)
+    lax.fori_loop(0, HEADS_HERE, scatter_head, 0)
 
     for h in range(HEADS_HERE):
         values[h, :, HEAD:] = jnp.ones((KEYS, HEAD), jnp.bfloat16)
@@ -172,9 +185,8 @@
         src = outs.at[
             h, pl.ds(pl.multiple_of(b * PAIR + ZS * ROWS + k * OUT_TEXT, 16), OUT_TEXT), :
         ]
-        px, pz = lax.rem(b * CORES + c, XS), (b * CORES + c) // XS
-        own = (px == x) & (pz == z) & (c == k)
-        return src, to.at[:, columns(x, z, h)], px, pz, own
+        px, pz = lax.rem(b, ZS) * CORES + k, b // ZS
+        return src, to.at[:, columns(x, z, h)], px, pz, (px == x) & (pz == z)
 
     def text_back(h, b, k):
         src, dst, px, pz, own = text_place(h, b, k)
@@ -183,10 +195,11 @@
             dst_ref=dst,
             send_sem=text_send.at[h],
             recv_sem=text_recv,
-            device_id=device(px, pz, k),
+            device_id=device(px, pz, c),
             device_id_type=MESH,
         )
 
+    length_copy.wait()
     to_sibling(0, keys, 0)
     to_sibling(1, values, 0)
 
@@ -194,9 +207,12 @@
         h, i = t // XS, lax.rem(t, XS)
         b = lax.rem(x + 1 + i, XS)
 
+        wait_for(
+            queries.at[h, pl.ds(pl.multiple_of(b * PAIR, 16), PAIR), :], query_recv.at[h, b]
+        )
+
         @pl.when(i == 0)
         def _():
-            wait_for(queries.at[h], recv.at[2, h])
             wait_for(keys.at[h, theirs, lanes], sib_recv.at[0, h])
             wait_for(values.at[h, theirs, lanes], sib_recv.at[1, h])
 
@@ -264,25 +280,48 @@
     wait_for(to, text_recv)
 
 
+def copy_out(video, text, video_out, text_out, sem):
+    copies = [pltpu.make_async_copy(text, text_out, sem.at[1])]
+    for i in range(CHIPS):
+        rows = pl.ds(i * (ROWS // CHIPS), ROWS // CHIPS)
+        copies.append(pltpu.make_async_copy(video.at[rows, :], video_out.at[rows, :], sem.at[0]))
+    for copy in copies:
+        copy.start()
+    for copy in copies:
+        copy.wait()
+
+
 def on_device(video_query, video_key, video_value, text_query, text_key, text_value, text_length):
-    any_spec = pl.BlockSpec(memory_space=pl.ANY)
+    any_spec = pl.BlockSpec(memory_space=pltpu.HBM)
     dma = pltpu.SemaphoreType.DMA
+    vmem_spec = pl.BlockSpec(memory_space=pltpu.VMEM)
     width = video_query.shape[1]
     flops = 4 * HEADS_HERE * XS * PAIR * KEYS * HEAD
-    return pl.pallas_call(
+    out_shape = (
+        pltpu.VMEM((ROWS, width), jnp.bfloat16),
+        pltpu.VMEM((OUT_TEXT, width), jnp.bfloat16),
+    )
+    inputs = [
+        pltpu.with_memory_space_constraint(a, pltpu.HBM)
+        for a in (video_query, video_key, video_value, text_query, text_key, text_value)
+    ]
+    video, text = pl.pallas_call(
         kernel,
-        out_shape=(
-            jax.ShapeDtypeStruct((ROWS, width), jnp.bfloat16),
-            jax.ShapeDtypeStruct((OUT_TEXT, width), jnp.bfloat16),
-        ),
-        in_specs=[pl.BlockSpec(memory_space=pltpu.SMEM)] + [any_spec] * 6,
-        out_specs=(any_spec, any_spec),
+        out_shape=out_shape,
+        in_specs=[any_spec] * 7,
+        out_specs=(vmem_spec, vmem_spec),
         scratch_shapes=[
             pltpu.VMEM((HEADS_HERE, KEYS, HEAD), jnp.bfloat16),
             pltpu.VMEM((HEADS_HERE, KEYS, 2 * HEAD), jnp.bfloat16),
             pltpu.VMEM((HEADS_HERE, XS * PAIR, HEAD), jnp.bfloat16),
             pltpu.VMEM((HEADS_HERE, XS * PAIR, HEAD), jnp.bfloat16),
-            dma((3, HEADS_HERE)),
+            pltpu.VMEM((OUT_TEXT, width), jnp.bfloat16),
+            pltpu.SMEM((1,), jnp.int32),
+            dma,
+            dma,
+            dma,
+            dma((2, HEADS_HERE)),
+            dma((HEADS_HERE, XS)),
             dma((3, HEADS_HERE)),
             dma((2, HEADS_HERE)),
             dma((2, HEADS_HERE)),
@@ -298,7 +337,18 @@
             collective_id=0, has_side_effects=True, vmem_limit_bytes=52 * 2**20
         ),
         name="joint_attention",
-    )(text_length, video_query, video_key, video_value, text_query, text_key, text_value)
+    )(text_length, *inputs)
+    return pl.pallas_call(
+        copy_out,
+        out_shape=(
+            jax.ShapeDtypeStruct((ROWS, width), jnp.bfloat16),
+            jax.ShapeDtypeStruct((OUT_TEXT, width), jnp.bfloat16),
+        ),
+        in_specs=[vmem_spec] * 2,
+        out_specs=(any_spec, any_spec),
+        scratch_shapes=[dma((2,))],
+        name="copy_out",
+    )(*(pltpu.with_memory_space_constraint(a, pltpu.VMEM) for a in (video, text)))
 
 
 def solution(mesh):

time: 88.4 us -> 83 us (0.939)
  local copies, waits for them, and re-layouts: 6.06 us -> 0 us
    unnamed x8 -> x0, local copies, waits for them, and re-layouts: 6.06 us -> none
    pallas_call x1 -> x2, Pallas kernels: 80.8 us -> 81.6 us  [the longest x1 80.4 us: on_device(): pl.pallas_call(kernel, out_shape=out_shape, in_specs=[any_spec] * 7, out_...]
where the time goes in v2:
time: 83 us; the launch traced here: 82.9 us
  Pallas kernels  81.6 us (98%)
  between operations  1.29 us (2%)
    pallas_call x1, Pallas kernels, on_device(): pl.pallas_call(kernel, out_shape=out_shape, in_specs=[any_spec] * 7, out_...  80.4 us

profile of v2, /device:TPU:22, one launch (start us, length us, event | category | flops | bytes accessed | tf_op | source)
XLA Modules:
  0.0 82.9 jit_solution(10138937081489148895)
XLA Ops:
  1.3 80.4 %joint_attention.1 = (bf16[256,3072]{1,0:T(8,128)(2,1)S(1)}, bf16[16,3072]{1,0:T(8,128)(2,1)S(1)}) custom-call(s32[1]{0:T(128)S(6)} %copy.9.length_in, bf16[256,3072]{1,0:T(8,128)(2,1)} %vq.1, bf16[256,3072]{1,0:T(8,128)(2,1)} %vk.1, bf16[256,3072]{1,0:T(8,128)(2,1)} %vv.1, bf16[32,3072]{1,0:T(8,128)(2,1)} %tq.1, bf16[32,3072]{1,0:T(8,128)(2,1)} %tk.1, ...), custom_call_target="tpu_custom_call" | custom-call | flops 14545846272 | bytes 6291456 | tf_op jit(solution)/shard_map/joint_attention/pallas_call | solution.py:308
  81.7 1.2 %copy_out.1 = (bf16[256,3072]{1,0:T(8,128)(2,1)}, bf16[16,3072]{1,0:T(8,128)(2,1)}) custom-call(bf16[256,3072]{1,0:T(8,128)(2,1)S(1)} %get-tuple-element.4.video, bf16[16,3072]{1,0:T(8,128)(2,1)S(1)} %get-tuple-element.5.text), custom_call_target="tpu_custom_call" | custom-call | tf_op jit(solution)/shard_map/copy_out/pallas_call | solution.py:341

commit v3 on v2

--- a/solution.py
+++ b/solution.py
@@ -17,12 +17,14 @@
 ROWS = 256
 TEXT_ROWS = 32
 OUT_TEXT = 16
-HALF = CHIPS * ROWS + XS * TEXT_ROWS
-KEYS = CORES * HALF
+KEYS = CORES * (CHIPS * ROWS + XS * TEXT_ROWS)
 PAIR = ZS * ROWS + TEXT_ROWS
 PEERS = ((1, 0), (3, 0), (2, 0), (0, 1), (1, 1), (3, 1), (2, 1))
 QUERY_PEERS = ((3, 0), (3, 1), (2, 0), (2, 1), (1, 0), (1, 1), (0, 1))
-VIDEO_1 = CHIPS * ROWS + CORES * XS * TEXT_ROWS
+PLANE = XS * ROWS
+TEXT_HERE = XS * TEXT_ROWS
+NEAR = PLANE + TEXT_HERE
+VIDEO_1 = CHIPS * ROWS + CORES * TEXT_HERE
 BLOCKS = (
     (CHIPS * ROWS, VIDEO_1),
     (0, 1024),
@@ -69,16 +71,20 @@
     def columns(px, pz, h):
         return pl.ds(pl.multiple_of(((px * ZS + pz) * HEADS_HERE + h) * HEAD, HEAD), HEAD)
 
-    chip = x * ZS + z
-    key_rows = pl.ds(pl.multiple_of(c * VIDEO_1 + chip * ROWS, 16), ROWS)
-    key_text = pl.ds(
-        pl.multiple_of(CHIPS * ROWS + c * (XS * TEXT_ROWS) + x * TEXT_ROWS, 16), TEXT_ROWS
+    key_rows = (
+        pl.ds(pl.multiple_of(PLANE + c * (VIDEO_1 - PLANE) + x * ROWS, 16), ROWS),
+        pl.ds(pl.multiple_of(c * (VIDEO_1 + PLANE) + x * ROWS, 16), ROWS),
     )
-    query_rows = pl.ds(pl.multiple_of(x * PAIR + z * ROWS, 16), ROWS)
+    key_text = pl.ds(pl.multiple_of(CHIPS * ROWS + c * TEXT_HERE + x * TEXT_ROWS, 16), TEXT_ROWS)
+    query_rows = tuple(pl.ds(pl.multiple_of(x * PAIR + dz * ROWS, 16), ROWS) for dz in (0, 1))
     own_text = pl.ds(pl.multiple_of(x * PAIR + ZS * ROWS + c * OUT_TEXT, 16), OUT_TEXT)
     other_text = pl.ds(pl.multiple_of(x * PAIR + ZS * ROWS + (1 - c) * OUT_TEXT, 16), OUT_TEXT)
-    mine = pl.ds(pl.multiple_of(c * HALF, 16), HALF)
-    theirs = pl.ds(pl.multiple_of((1 - c) * HALF, 16), HALF)
+
+    def key_piece(pc, far):
+        if far:
+            return pl.ds(pl.multiple_of(pc * (VIDEO_1 + PLANE), 16), PLANE)
+        return pl.ds(pl.multiple_of(PLANE + pc * NEAR, 16), NEAR)
+
     lanes = pl.ds(0, HEAD)
 
     stage = pltpu.make_async_remote_copy(
@@ -91,36 +97,41 @@
     )
     stage.start()
 
-    def scatter(h, pieces, dst, sems, peers):
+    def scatter(h, pieces, dst, sems, peers, own=True, rows=None):
         for dx, dz in peers:
             px, pz = lax.rem(x + dx, XS), lax.rem(z + dz, ZS)
             pltpu.make_async_remote_copy(
                 src_ref=pieces.at[:, columns(px, pz, h)],
-                dst_ref=dst,
+                dst_ref=dst if rows is None else dst.at[rows[dz], :],
                 send_sem=sems[0],
                 recv_sem=sems[1],
                 device_id=device(px, pz, c),
                 device_id_type=MESH,
             ).start()
-        pltpu.make_async_copy(pieces.at[:, columns(x, z, h)], dst, sems[1]).start()
-
-    text_peers = tuple(p for p in PEERS if p[1] == 0)
+        if own:
+            place = dst if rows is None else dst.at[rows[0], :]
+            pltpu.make_async_copy(pieces.at[:, columns(x, z, h)], place, sems[1]).start()
+
+    near = tuple(p for p in PEERS if p[1] == 0)
+    far = tuple(p for p in PEERS if p[1] == 1)
     tq_own = tq.at[pl.ds(pl.multiple_of(c * OUT_TEXT, 16), OUT_TEXT), :]
 
     def scatter_head(h, carry):
         for i, (video, text, place) in enumerate(((vk, tk, keys), (vv, tv, values))):
-            sems = send.at[i, h], recv.at[i, h]
-            scatter(h, video, place.at[h, key_rows, lanes], sems, PEERS)
-            scatter(h, text, place.at[h, key_text, lanes], sems, text_peers)
+            sems = send.at[i, h], recv.at[i, h, 0]
+            scatter(h, video, place.at[h, key_rows[0], lanes], sems, near)
+            scatter(h, text, place.at[h, key_text, lanes], sems, near)
+            sems = send.at[i, h], recv.at[i, h, 1]
+            scatter(h, video, place.at[h, key_rows[1], lanes], sems, far, own=False)
         sems = send.at[2, h], query_recv.at[h, x]
-        scatter(h, vq, queries.at[h, query_rows, :], sems, QUERY_PEERS)
+        scatter(h, vq, queries.at[h], sems, QUERY_PEERS, rows=query_rows)
 
         @pl.when(h == 0)
         def _():
             stage.wait()
 
-        scatter(h, tq_own, queries.at[h, own_text, :], sems, text_peers)
-        scatter(h, staged, queries.at[h, other_text, :], sems, text_peers)
+        scatter(h, tq_own, queries.at[h, own_text, :], sems, near)
+        scatter(h, staged, queries.at[h, other_text, :], sems, near)
         return carry
 
     lax.fori_loop(0, HEADS_HERE, scatter_head, 0)
@@ -128,19 +139,20 @@
     for h in range(HEADS_HERE):
         values[h, :, HEAD:] = jnp.ones((KEYS, HEAD), jnp.bfloat16)
 
-    def to_sibling(i, place, h):
-        wait_for(place.at[h, mine, lanes], recv.at[i, h])
+    def to_sibling(i, place, h, far):
+        rows = key_piece(c, far)
+        wait_for(place.at[h, rows, lanes], recv.at[i, h, far])
         pltpu.make_async_remote_copy(
-            src_ref=place.at[h, mine, lanes],
-            dst_ref=place.at[h, mine, lanes],
-            send_sem=sib_send.at[i, h],
-            recv_sem=sib_recv.at[i, h],
+            src_ref=place.at[h, rows, lanes],
+            dst_ref=place.at[h, rows, lanes],
+            send_sem=sib_send.at[i, h, far],
+            recv_sem=sib_recv.at[i, h, far],
             device_id=device(x, z, 1 - c),
             device_id_type=MESH,
         ).start()
 
-    def attend(h, b):
-        rows = pl.ds(pl.multiple_of(b * PAIR, 16), PAIR)
+    def attend(h, b, first=0, count=PAIR):
+        rows = pl.ds(pl.multiple_of(b * PAIR + first, 16), count)
         q = queries[h, rows, :]
         t = lax.broadcasted_iota(jnp.int32, (1, CORES * XS * TEXT_ROWS), 1)
         part = XS * TEXT_ROWS
@@ -171,9 +183,10 @@
                 scores = following
         outs[h, rows, :] = (summed[:, :HEAD] / summed[:, HEAD:]).astype(jnp.bfloat16)
 
-    def video_back(h, b, pz):
+    def video_back(h, b, dz):
+        pz = lax.rem(z + dz, ZS)
         return pltpu.make_async_remote_copy(
-            src_ref=outs.at[h, pl.ds(pl.multiple_of(b * PAIR + pz * ROWS, 16), ROWS), :],
+            src_ref=outs.at[h, pl.ds(pl.multiple_of(b * PAIR + dz * ROWS, 16), ROWS), :],
             dst_ref=vo.at[:, columns(x, z, h)],
             send_sem=out_send.at[h],
             recv_sem=out_recv,
@@ -200,8 +213,39 @@
         )
 
     length_copy.wait()
-    to_sibling(0, keys, 0)
-    to_sibling(1, values, 0)
+    for i, place in ((0, keys), (1, values)):
+        for part in range(2):
+            to_sibling(i, place, 0, part)
+
+    def near_back(h, i, b):
+        @pl.when(i < XS - 1)
+        def _():
+            video_back(h, b, 0).start()
+
+        @pl.when(i == XS - 1)
+        def _():
+            pltpu.make_async_copy(
+                outs.at[h, query_rows[0], :], vo.at[:, columns(x, z, h)], out_recv
+            ).start()
+
+    def far_back(h, b):
+        video_back(h, b, 1).start()
+
+        for k in range(CORES):
+            own, copy = text_back(h, b, k)
+            src, dst, _, _, _ = text_place(h, b, k)
+
+            @pl.when(own)
+            def _():
+                pltpu.make_async_copy(src, dst, text_recv).start()
+
+            @pl.when(jnp.logical_not(own))
+            def _():
+                copy.start()
+
+    def give_back(h, i, b):
+        far_back(h, b)
+        near_back(h, i, b)
 
     def turn(t, carry):
         h, i = t // XS, lax.rem(t, XS)
@@ -213,46 +257,47 @@
 
         @pl.when(i == 0)
         def _():
-            wait_for(keys.at[h, theirs, lanes], sib_recv.at[0, h])
-            wait_for(values.at[h, theirs, lanes], sib_recv.at[1, h])
+            for part in range(2):
+                rows = key_piece(1 - c, part)
+                wait_for(keys.at[h, rows, lanes], sib_recv.at[0, h, part])
+                wait_for(values.at[h, rows, lanes], sib_recv.at[1, h, part])
+
+        @pl.when((i == XS - 2) & (h < HEADS_HERE - 1))
+        def _():
+            to_sibling(0, keys, h + 1, 0)
+            to_sibling(0, keys, h + 1, 1)
+
+
+        last = t == HEADS_HERE * XS - 1
+
+        @pl.when(jnp.logical_not(last))
+        def _():
+            attend(h, b)
+
+        @pl.when(last)
+        def _():
+            attend(h, b, ROWS, PAIR - ROWS)
+            far_back(h, b)
+            attend(h, b, 0, ROWS)
+            near_back(h, i, b)
+
+        @pl.when((h == HEADS_HERE - 1) & jnp.logical_not(last))
+        def _():
+            give_back(h, i, b)
 
         @pl.when((i == XS - 1) & (h < HEADS_HERE - 1))
         def _():
-            to_sibling(0, keys, h + 1)
-
-        attend(h, b)
-
-        for dz in (1, 0):
-            pz = lax.rem(z + dz, ZS)
-            if dz == 1:
-                video_back(h, b, pz).start()
-            else:
-
-                @pl.when(i < XS - 1)
-                def _():
-                    video_back(h, b, pz).start()
-
-                @pl.when(i == XS - 1)
-                def _():
-                    pltpu.make_async_copy(
-                        outs.at[h, query_rows, :], vo.at[:, columns(x, z, h)], out_recv
-                    ).start()
-
-        for k in range(CORES):
-            own, copy = text_back(h, b, k)
-            src, dst, _, _, _ = text_place(h, b, k)
-
-            @pl.when(own)
-            def _():
-                pltpu.make_async_copy(src, dst, text_recv).start()
-
-            @pl.when(jnp.logical_not(own))
-            def _():
-                copy.start()
-
-        @pl.when((i == XS - 1) & (h < HEADS_HERE - 1))
-        def _():
-            to_sibling(1, values, h + 1)
+            to_sibling(1, values, h + 1, 0)
+            to_sibling(1, values, h + 1, 1)
+
+        @pl.when((h == HEADS_HERE - 2) & (i == XS - 1))
+        def _():
+            def early(n, carry):
+                ii = lax.rem(n, XS)
+                give_back(n // XS, ii, lax.rem(x + 1 + ii, XS))
+                return carry
+
+            lax.fori_loop(0, (HEADS_HERE - 1) * XS, early, 0)
 
         return carry
 
@@ -263,7 +308,8 @@
             sent = (CHIPS - 1) * ROWS + (XS - 1) * TEXT_ROWS
             wait_for(outs.at[h, pl.ds(0, sent), :], send.at[i, h])
         for i, place in ((0, keys), (1, values)):
-            wait_for(place.at[h, mine, lanes], sib_send.at[i, h])
+            for part in range(2):
+                wait_for(place.at[h, key_piece(c, part), lanes], sib_send.at[i, h, part])
         wait_for(outs.at[h, pl.ds(0, (CHIPS - 1) * ROWS), :], out_send.at[h])
         for b in range(XS):
             for k in range(CORES):
@@ -320,11 +366,11 @@
             dma,
             dma,
             dma,
-            dma((2, HEADS_HERE)),
+            dma((2, HEADS_HERE, 2)),
             dma((HEADS_HERE, XS)),
             dma((3, HEADS_HERE)),
-            dma((2, HEADS_HERE)),
-            dma((2, HEADS_HERE)),
+            dma((2, HEADS_HERE, 2)),
+            dma((2, HEADS_HERE, 2)),
             dma,
             dma((HEADS_HERE,)),
             dma,

time: 83 us -> 82.5 us (level)
  Pallas kernels: 81.6 us -> 80.4 us
    pallas_call x1, Pallas kernels: 80.4 us -> 79.2 us  [on_device(): pl.pallas_call(kernel, out_shape=out_shape, in_specs=[any_spec] * 7, out_...]
where the time goes in v3:
time: 82.5 us; the launch traced here: 81.7 us
  Pallas kernels  80.4 us (97%)
  between operations  1.29 us (2%)
    pallas_call x1, Pallas kernels, on_device(): pl.pallas_call(kernel, out_shape=out_shape, in_specs=[any_spec] * 7, out_...  79.2 us

profile of v3, /device:TPU:22, one launch (start us, length us, event | category | flops | bytes accessed | tf_op | source)
XLA Modules:
  0.0 81.7 jit_solution(6697276733580833600)
XLA Ops:
  1.3 79.2 %joint_attention.1 = (bf16[256,3072]{1,0:T(8,128)(2,1)S(1)}, bf16[16,3072]{1,0:T(8,128)(2,1)S(1)}) custom-call(s32[1]{0:T(128)S(6)} %copy.9.length_in, bf16[256,3072]{1,0:T(8,128)(2,1)} %vq.1, bf16[256,3072]{1,0:T(8,128)(2,1)} %vk.1, bf16[256,3072]{1,0:T(8,128)(2,1)} %vv.1, bf16[32,3072]{1,0:T(8,128)(2,1)} %tq.1, bf16[32,3072]{1,0:T(8,128)(2,1)} %tk.1, ...), custom_call_target="tpu_custom_call" | custom-call | flops 14545846272 | bytes 6291456 | tf_op jit(solution)/shard_map/joint_attention/pallas_call | solution.py:354
  80.5 1.2 %copy_out.1 = (bf16[256,3072]{1,0:T(8,128)(2,1)}, bf16[16,3072]{1,0:T(8,128)(2,1)}) custom-call(bf16[256,3072]{1,0:T(8,128)(2,1)S(1)} %get-tuple-element.4.video, bf16[16,3072]{1,0:T(8,128)(2,1)S(1)} %get-tuple-element.5.text), custom_call_target="tpu_custom_call" | custom-call | tf_op jit(solution)/shard_map/copy_out/pallas_call | solution.py:387

commit v4 on v3

--- a/solution.py
+++ b/solution.py
@@ -17,21 +17,14 @@
 ROWS = 256
 TEXT_ROWS = 32
 OUT_TEXT = 16
-KEYS = CORES * (CHIPS * ROWS + XS * TEXT_ROWS)
+KEYS = CORES * CHIPS * ROWS
 PAIR = ZS * ROWS + TEXT_ROWS
 PEERS = ((1, 0), (3, 0), (2, 0), (0, 1), (1, 1), (3, 1), (2, 1))
 QUERY_PEERS = ((3, 0), (3, 1), (2, 0), (2, 1), (1, 0), (1, 1), (0, 1))
 PLANE = XS * ROWS
+VIDEO_PAIR = ZS * ROWS
 TEXT_HERE = XS * TEXT_ROWS
-NEAR = PLANE + TEXT_HERE
-VIDEO_1 = CHIPS * ROWS + CORES * TEXT_HERE
-BLOCKS = (
-    (CHIPS * ROWS, VIDEO_1),
-    (0, 1024),
-    (1024, 2048),
-    (VIDEO_1, VIDEO_1 + 1024),
-    (VIDEO_1 + 1024, VIDEO_1 + 2048),
-)
+WIDTH = HEADS_HERE * HEAD
 
 
 def dot(a, b, dims):
@@ -44,7 +37,9 @@
 
 def kernel(
     length_in, vq, vk, vv, tq, tk, tv, vo, to,
-    keys, values, queries, outs, staged, length, length_sem, stage_send, stage_recv,
+    keys, values, queries, outs, text_keys, text_values, text_queries, staged,
+    length, length_sem, stage_send, stage_recv, stage_own,
+    words_recv, words_send, words_sib_recv, words_sib_send,
     recv, query_recv, send, sib_recv, sib_send, out_recv, out_send, text_recv, text_send,
 ):
     u = lax.axis_index("ulysses")
@@ -71,67 +66,101 @@
     def columns(px, pz, h):
         return pl.ds(pl.multiple_of(((px * ZS + pz) * HEADS_HERE + h) * HEAD, HEAD), HEAD)
 
-    key_rows = (
-        pl.ds(pl.multiple_of(PLANE + c * (VIDEO_1 - PLANE) + x * ROWS, 16), ROWS),
-        pl.ds(pl.multiple_of(c * (VIDEO_1 + PLANE) + x * ROWS, 16), ROWS),
+    def word_columns(px, pz):
+        return pl.ds(pl.multiple_of((px * ZS + pz) * WIDTH, HEAD), WIDTH)
+
+    key_rows = tuple(
+        pl.ds(pl.multiple_of((c * ZS + far) * PLANE + x * ROWS, 16), ROWS) for far in (0, 1)
     )
-    key_text = pl.ds(pl.multiple_of(CHIPS * ROWS + c * TEXT_HERE + x * TEXT_ROWS, 16), TEXT_ROWS)
-    query_rows = tuple(pl.ds(pl.multiple_of(x * PAIR + dz * ROWS, 16), ROWS) for dz in (0, 1))
-    own_text = pl.ds(pl.multiple_of(x * PAIR + ZS * ROWS + c * OUT_TEXT, 16), OUT_TEXT)
-    other_text = pl.ds(pl.multiple_of(x * PAIR + ZS * ROWS + (1 - c) * OUT_TEXT, 16), OUT_TEXT)
+    key_words = pl.ds(pl.multiple_of(c * TEXT_HERE + x * TEXT_ROWS, 16), TEXT_ROWS)
+    words_mine = pl.ds(pl.multiple_of(c * TEXT_HERE, 16), TEXT_HERE)
+    words_theirs = pl.ds(pl.multiple_of((1 - c) * TEXT_HERE, 16), TEXT_HERE)
+    query_rows = tuple(
+        pl.ds(pl.multiple_of(x * VIDEO_PAIR + far * ROWS, 16), ROWS) for far in (0, 1)
+    )
+    query_words = pl.ds(pl.multiple_of(x * TEXT_ROWS, 16), TEXT_ROWS)
 
     def key_piece(pc, far):
-        if far:
-            return pl.ds(pl.multiple_of(pc * (VIDEO_1 + PLANE), 16), PLANE)
-        return pl.ds(pl.multiple_of(PLANE + pc * NEAR, 16), NEAR)
+        return pl.ds(pl.multiple_of((pc * ZS + far) * PLANE, 16), PLANE)
 
     lanes = pl.ds(0, HEAD)
 
+    def half(k):
+        return pl.ds(pl.multiple_of(k * OUT_TEXT, 16), OUT_TEXT)
+
     stage = pltpu.make_async_remote_copy(
-        src_ref=tq.at[pl.ds(pl.multiple_of((1 - c) * OUT_TEXT, 16), OUT_TEXT), :],
-        dst_ref=staged,
+        src_ref=tq.at[half(1 - c), :],
+        dst_ref=staged.at[half(c), :],
         send_sem=stage_send,
         recv_sem=stage_recv,
         device_id=device(x, z, 1 - c),
         device_id_type=MESH,
     )
     stage.start()
-
-    def scatter(h, pieces, dst, sems, peers, own=True, rows=None):
+    stay = pltpu.make_async_copy(tq.at[half(c), :], staged.at[half(c), :], stage_own)
+    stay.start()
+
+    def scatter(h, pieces, place, rows, sems, peers):
         for dx, dz in peers:
             px, pz = lax.rem(x + dx, XS), lax.rem(z + dz, ZS)
             pltpu.make_async_remote_copy(
                 src_ref=pieces.at[:, columns(px, pz, h)],
-                dst_ref=dst if rows is None else dst.at[rows[dz], :],
+                dst_ref=place.at[h, rows[dz], lanes],
                 send_sem=sems[0],
                 recv_sem=sems[1],
                 device_id=device(px, pz, c),
                 device_id_type=MESH,
             ).start()
-        if own:
-            place = dst if rows is None else dst.at[rows[0], :]
-            pltpu.make_async_copy(pieces.at[:, columns(x, z, h)], place, sems[1]).start()
+
+    def stays(h, pieces, place, rows, sem):
+        pltpu.make_async_copy(
+            pieces.at[:, columns(x, z, h)], place.at[h, rows[0], lanes], sem
+        ).start()
 
     near = tuple(p for p in PEERS if p[1] == 0)
     far = tuple(p for p in PEERS if p[1] == 1)
-    tq_own = tq.at[pl.ds(pl.multiple_of(c * OUT_TEXT, 16), OUT_TEXT), :]
+
+    def scatter_words(i, pieces, place, rows):
+        for dx, _ in near:
+            px = lax.rem(x + dx, XS)
+            pltpu.make_async_remote_copy(
+                src_ref=pieces.at[:, word_columns(px, z)],
+                dst_ref=place.at[rows, :],
+                send_sem=words_send.at[i],
+                recv_sem=words_recv.at[i],
+                device_id=device(px, z, c),
+                device_id_type=MESH,
+            ).start()
+        pltpu.make_async_copy(
+            pieces.at[:, word_columns(x, z)], place.at[rows, :], words_recv.at[i]
+        ).start()
 
     def scatter_head(h, carry):
-        for i, (video, text, place) in enumerate(((vk, tk, keys), (vv, tv, values))):
-            sems = send.at[i, h], recv.at[i, h, 0]
-            scatter(h, video, place.at[h, key_rows[0], lanes], sems, near)
-            scatter(h, text, place.at[h, key_text, lanes], sems, near)
-            sems = send.at[i, h], recv.at[i, h, 1]
-            scatter(h, video, place.at[h, key_rows[1], lanes], sems, far, own=False)
+        for i, (video, place) in enumerate(((vk, keys), (vv, values))):
+            scatter(h, video, place, key_rows, (send.at[i, h], recv.at[i, h, 0]), near)
+            scatter(h, video, place, key_rows, (send.at[i, h], recv.at[i, h, 1]), far)
+            stays(h, video, place, key_rows, recv.at[i, h, 0])
+
+        @pl.when(h == 0)
+        def _():
+            scatter_words(0, tk, text_keys, key_words)
+            scatter_words(1, tv, text_values, key_words)
+            stay.wait()
+            stage.wait()
+            scatter_words(2, staged, text_queries, query_words)
+
         sems = send.at[2, h], query_recv.at[h, x]
-        scatter(h, vq, queries.at[h], sems, QUERY_PEERS, rows=query_rows)
-
-        @pl.when(h == 0)
-        def _():
-            stage.wait()
-
-        scatter(h, tq_own, queries.at[h, own_text, :], sems, near)
-        scatter(h, staged, queries.at[h, other_text, :], sems, near)
+        scatter(h, vq, queries, query_rows, sems, QUERY_PEERS[:-3])
+
+        @pl.when(x == 0)
+        def _():
+            scatter(h, vq, queries, query_rows, sems, QUERY_PEERS[-1:] + QUERY_PEERS[-3:-1])
+
+        @pl.when(x > 0)
+        def _():
+            scatter(h, vq, queries, query_rows, sems, QUERY_PEERS[-3:])
+
+        stays(h, vq, queries, query_rows, query_recv.at[h, x])
         return carry
 
     lax.fori_loop(0, HEADS_HERE, scatter_head, 0)
@@ -151,36 +180,50 @@
             device_id_type=MESH,
         ).start()
 
+    def words_to_sibling(i, place):
+        wait_for(place.at[words_mine, :], words_recv.at[i])
+        pltpu.make_async_remote_copy(
+            src_ref=place.at[words_mine, :],
+            dst_ref=place.at[words_mine, :],
+            send_sem=words_sib_send.at[i],
+            recv_sem=words_sib_recv.at[i],
+            device_id=device(x, z, 1 - c),
+            device_id_type=MESH,
+        ).start()
+
     def attend(h, b, first=0, count=PAIR):
-        rows = pl.ds(pl.multiple_of(b * PAIR + first, 16), count)
-        q = queries[h, rows, :]
-        t = lax.broadcasted_iota(jnp.int32, (1, CORES * XS * TEXT_ROWS), 1)
-        part = XS * TEXT_ROWS
+        head = pl.ds(pl.multiple_of(h * HEAD, HEAD), HEAD)
+        video = min(first + count, VIDEO_PAIR) - first
+        q = queries[h, pl.ds(pl.multiple_of(b * VIDEO_PAIR + first, 16), video), :]
+        if first + count > VIDEO_PAIR:
+            words = text_queries[pl.ds(pl.multiple_of(b * TEXT_ROWS, 16), TEXT_ROWS), head]
+            q = jnp.concatenate([q, words], axis=0)
+        t = lax.broadcasted_iota(jnp.int32, (1, CORES * TEXT_HERE), 1)
         position = (
-            (lax.rem(t, part) // TEXT_ROWS) * (CORES * TEXT_ROWS)
-            + (t // part) * TEXT_ROWS
+            (lax.rem(t, TEXT_HERE) // TEXT_ROWS) * (CORES * TEXT_ROWS)
+            + (t // TEXT_HERE) * TEXT_ROWS
             + lax.rem(t, TEXT_ROWS)
         )
-        valid = position < length[0]
+        scores = dot(q, text_keys[:, head], ((1,), (1,)))
+        scores = jnp.where(position < length[0], scores, NEG_BIG)
+        ones = jnp.ones((CORES * TEXT_HERE, HEAD), jnp.bfloat16)
+        block = jnp.concatenate([text_values[:, head], ones], axis=1)
         top = None
-        first, last = BLOCKS[0]
-        scores = dot(q, keys[h, first:last, :], ((1,), (1,)))
-        scores = jnp.where(valid, scores, NEG_BIG)
-        for j, (first, last) in enumerate(BLOCKS):
-            if j + 1 < len(BLOCKS):
-                lo, hi = BLOCKS[j + 1]
-                following = dot(q, keys[h, lo:hi, :], ((1,), (1,)))
+        for lo in range(0, KEYS + 1, PLANE):
+            if lo < KEYS:
+                following = dot(q, keys[h, lo : lo + PLANE, :], ((1,), (1,)))
             here = jnp.max(scores, axis=1, keepdims=True)
             new_top = here if top is None else jnp.maximum(top, here)
             weights = jnp.exp2(scores * SCALE - new_top * SCALE).astype(jnp.bfloat16)
-            product = dot(weights, values[h, first:last, :], ((1,), (0,)))
+            product = dot(weights, block, ((1,), (0,)))
             if top is None:
                 summed = product
             else:
                 summed = summed * jnp.exp2((top - new_top) * SCALE) + product
             top = new_top
-            if j + 1 < len(BLOCKS):
-                scores = following
+            if lo < KEYS:
+                scores, block = following, values[h, lo : lo + PLANE, :]
+        rows = pl.ds(pl.multiple_of(b * PAIR + first, 16), count)
         outs[h, rows, :] = (summed[:, :HEAD] / summed[:, HEAD:]).astype(jnp.bfloat16)
 
     def video_back(h, b, dz):
@@ -216,16 +259,23 @@
     for i, place in ((0, keys), (1, values)):
         for part in range(2):
             to_sibling(i, place, 0, part)
-
-    def near_back(h, i, b):
-        @pl.when(i < XS - 1)
+    words_to_sibling(0, text_keys)
+    words_to_sibling(1, text_values)
+    wait_for(text_queries, words_recv.at[2])
+    for i, place in ((0, text_keys), (1, text_values)):
+        wait_for(place.at[words_theirs, :], words_sib_recv.at[i])
+
+    def near_back(h, b):
+        @pl.when(b != x)
         def _():
             video_back(h, b, 0).start()
 
-        @pl.when(i == XS - 1)
+        @pl.when(b == x)
         def _():
             pltpu.make_async_copy(
-                outs.at[h, query_rows[0], :], vo.at[:, columns(x, z, h)], out_recv
+                outs.at[h, pl.ds(pl.multiple_of(x * PAIR, 16), ROWS), :],
+                vo.at[:, columns(x, z, h)],
+                out_recv,
             ).start()
 
     def far_back(h, b):
@@ -243,16 +293,20 @@
             def _():
                 copy.start()
 
-    def give_back(h, i, b):
+    def give_back(h, b):
         far_back(h, b)
-        near_back(h, i, b)
+        near_back(h, b)
+
+    def place_of(i):
+        late = (x == 0) & (i >= XS - 2)
+        return lax.rem(x + 1 + jnp.where(late, 2 * XS - 3 - i, i), XS)
 
     def turn(t, carry):
         h, i = t // XS, lax.rem(t, XS)
-        b = lax.rem(x + 1 + i, XS)
+        b = place_of(i)
 
         wait_for(
-            queries.at[h, pl.ds(pl.multiple_of(b * PAIR, 16), PAIR), :], query_recv.at[h, b]
+            queries.at[h, pl.ds(pl.multiple_of(b * VIDEO_PAIR, 16), VIDEO_PAIR), :], query_recv.at[h, b]
         )
 
         @pl.when(i == 0)
@@ -279,25 +333,26 @@
             attend(h, b, ROWS, PAIR - ROWS)
             far_back(h, b)
             attend(h, b, 0, ROWS)
-            near_back(h, i, b)
+            near_back(h, b)
 
         @pl.when((h == HEADS_HERE - 1) & jnp.logical_not(last))
         def _():
-            give_back(h, i, b)
+            give_back(h, b)
 
         @pl.when((i == XS - 1) & (h < HEADS_HERE - 1))
         def _():
             to_sibling(1, values, h + 1, 0)
             to_sibling(1, values, h + 1, 1)
 
-        @pl.when((h == HEADS_HERE - 2) & (i == XS - 1))
-        def _():
-            def early(n, carry):
-                ii = lax.rem(n, XS)
-                give_back(n // XS, ii, lax.rem(x + 1 + ii, XS))
-                return carry
-
-            lax.fori_loop(0, (HEADS_HERE - 1) * XS, early, 0)
+        for done in range(HEADS_HERE - 1):
+
+            @pl.when(t == (HEADS_HERE - 1) * XS - 1 + c * done)
+            def _():
+                def early(ii, carry):
+                    give_back(done, place_of(ii))
+                    return carry
+
+                lax.fori_loop(0, XS, early, 0)
 
         return carry
 
@@ -305,8 +360,7 @@
 
     def finish(h, carry):
         for i in range(3):
-            sent = (CHIPS - 1) * ROWS + (XS - 1) * TEXT_ROWS
-            wait_for(outs.at[h, pl.ds(0, sent), :], send.at[i, h])
+            wait_for(outs.at[h, pl.ds(0, (CHIPS - 1) * ROWS), :], send.at[i, h])
         for i, place in ((0, keys), (1, values)):
             for part in range(2):
                 wait_for(place.at[h, key_piece(c, part), lanes], sib_send.at[i, h, part])
@@ -322,6 +376,10 @@
         return carry
 
     lax.fori_loop(0, HEADS_HERE, finish, 0)
+    for i in range(3):
+        wait_for(text_keys.at[pl.ds(0, (XS - 1) * TEXT_ROWS), :], words_send.at[i])
+    for i, place in ((0, text_keys), (1, text_values)):
+        wait_for(place.at[words_mine, :], words_sib_send.at[i])
     wait_for(vo, out_recv)
     wait_for(to, text_recv)
 
@@ -342,7 +400,7 @@
     dma = pltpu.SemaphoreType.DMA
     vmem_spec = pl.BlockSpec(memory_space=pltpu.VMEM)
     width = video_query.shape[1]
-    flops = 4 * HEADS_HERE * XS * PAIR * KEYS * HEAD
+    flops = 4 * HEADS_HERE * XS * PAIR * (KEYS + CORES * TEXT_HERE) * HEAD
     out_shape = (
         pltpu.VMEM((ROWS, width), jnp.bfloat16),
         pltpu.VMEM((OUT_TEXT, width), jnp.bfloat16),
@@ -359,13 +417,21 @@
         scratch_shapes=[
             pltpu.VMEM((HEADS_HERE, KEYS, HEAD), jnp.bfloat16),
             pltpu.VMEM((HEADS_HERE, KEYS, 2 * HEAD), jnp.bfloat16),
+            pltpu.VMEM((HEADS_HERE, XS * VIDEO_PAIR, HEAD), jnp.bfloat16),
             pltpu.VMEM((HEADS_HERE, XS * PAIR, HEAD), jnp.bfloat16),
-            pltpu.VMEM((HEADS_HERE, XS * PAIR, HEAD), jnp.bfloat16),
-            pltpu.VMEM((OUT_TEXT, width), jnp.bfloat16),
+            pltpu.VMEM((CORES * TEXT_HERE, WIDTH), jnp.bfloat16),
+            pltpu.VMEM((CORES * TEXT_HERE, WIDTH), jnp.bfloat16),
+            pltpu.VMEM((TEXT_HERE, WIDTH), jnp.bfloat16),
+            pltpu.VMEM((TEXT_ROWS, width), jnp.bfloat16),
             pltpu.SMEM((1,), jnp.int32),
             dma,
             dma,
             dma,
+            dma,
+            dma((3,)),
+            dma((3,)),
+            dma((2,)),
+            dma((2,)),
             dma((2, HEADS_HERE, 2)),
             dma((HEADS_HERE, XS)),
             dma((3, HEADS_HERE)),

time: 82.5 us -> 82 us (level)
  Pallas kernels: 80.4 us -> 79.3 us
    pallas_call x1, Pallas kernels: 79.2 us -> 78.1 us  [on_device(): pl.pallas_call(kernel, out_shape=out_shape, in_specs=[any_spec] * 7, out_...]
where the time goes in v4:
time: 82 us; the launch traced here: 80.6 us
  Pallas kernels  79.3 us (97%)
  between operations  1.29 us (2%)
    pallas_call x1, Pallas kernels, on_device(): pl.pallas_call(kernel, out_shape=out_shape, in_specs=[any_spec] * 7, out_...  78.1 us

profile of v4, /device:TPU:22, one launch (start us, length us, event | category | flops | bytes accessed | tf_op | source)
XLA Modules:
  0.0 80.6 jit_solution(3018375371277876044)
XLA Ops:
  1.3 78.1 %joint_attention.1 = (bf16[256,3072]{1,0:T(8,128)(2,1)S(1)}, bf16[16,3072]{1,0:T(8,128)(2,1)S(1)}) custom-call(s32[1]{0:T(128)S(6)} %copy.9.length_in, bf16[256,3072]{1,0:T(8,128)(2,1)} %vq.1, bf16[256,3072]{1,0:T(8,128)(2,1)} %vk.1, bf16[256,3072]{1,0:T(8,128)(2,1)} %vv.1, bf16[32,3072]{1,0:T(8,128)(2,1)} %tq.1, bf16[32,3072]{1,0:T(8,128)(2,1)} %tk.1, ...), custom_call_target="tpu_custom_call" | custom-call | flops 14545846272 | bytes 6291456 | tf_op jit(solution)/shard_map/joint_attention/pallas_call | solution.py:412
  79.4 1.2 %copy_out.1 = (bf16[256,3072]{1,0:T(8,128)(2,1)}, bf16[16,3072]{1,0:T(8,128)(2,1)}) custom-call(bf16[256,3072]{1,0:T(8,128)(2,1)S(1)} %get-tuple-element.4.video, bf16[16,3072]{1,0:T(8,128)(2,1)S(1)} %get-tuple-element.5.text), custom_call_target="tpu_custom_call" | custom-call | tf_op jit(solution)/shard_map/copy_out/pallas_call | solution.py:453

commit v5 on v4

--- a/solution.py
+++ b/solution.py
@@ -101,7 +101,9 @@
     stay.start()
 
     def scatter(h, pieces, place, rows, sems, peers):
-        for dx, dz in peers:
+        for (dx, dz), (other, _) in zip(peers, peers[::-1]):
+            if all(p[1] == dz for p in peers):
+                dx = jnp.where(c == 0, dx, other)
             px, pz = lax.rem(x + dx, XS), lax.rem(z + dz, ZS)
             pltpu.make_async_remote_copy(
                 src_ref=pieces.at[:, columns(px, pz, h)],

time: 82 us -> 81.8 us (level); the launches traced: 80.6 us -> 81.5 us
  Pallas kernels: 79.3 us -> 80.2 us
    pallas_call x1, Pallas kernels: 78.1 us -> 79 us  [on_device(): pl.pallas_call(kernel, out_shape=out_shape, in_specs=[any_spec] * 7, out_...]
where the time goes in v5:
time: 81.8 us; the launch traced here: 81.5 us
  Pallas kernels  80.2 us (98%)
  between operations  1.29 us (2%)
    pallas_call x1, Pallas kernels, on_device(): pl.pallas_call(kernel, out_shape=out_shape, in_specs=[any_spec] * 7, out_...  79 us

profile of v5, /device:TPU:22, one launch (start us, length us, event | category | flops | bytes accessed | tf_op | source)
XLA Modules:
  0.0 81.5 jit_solution(6188958406642808320)
XLA Ops:
  1.3 79.0 %joint_attention.1 = (bf16[256,3072]{1,0:T(8,128)(2,1)S(1)}, bf16[16,3072]{1,0:T(8,128)(2,1)S(1)}) custom-call(s32[1]{0:T(128)S(6)} %copy.9.length_in, bf16[256,3072]{1,0:T(8,128)(2,1)} %vq.1, bf16[256,3072]{1,0:T(8,128)(2,1)} %vk.1, bf16[256,3072]{1,0:T(8,128)(2,1)} %vv.1, bf16[32,3072]{1,0:T(8,128)(2,1)} %tq.1, bf16[32,3072]{1,0:T(8,128)(2,1)} %tk.1, ...), custom_call_target="tpu_custom_call" | custom-call | flops 14545846272 | bytes 6291456 | tf_op jit(solution)/shard_map/joint_attention/pallas_call | solution.py:414
  80.3 1.2 %copy_out.1 = (bf16[256,3072]{1,0:T(8,128)(2,1)}, bf16[16,3072]{1,0:T(8,128)(2,1)}) custom-call(bf16[256,3072]{1,0:T(8,128)(2,1)S(1)} %get-tuple-element.4.video, bf16[16,3072]{1,0:T(8,128)(2,1)S(1)} %get-tuple-element.5.text), custom_call_target="tpu_custom_call" | custom-call | tf_op jit(solution)/shard_map/copy_out/pallas_call | solution.py:455

commit v6 on v4

--- a/solution.py
+++ b/solution.py
@@ -198,13 +198,18 @@
         if first + count > VIDEO_PAIR:
             words = text_queries[pl.ds(pl.multiple_of(b * TEXT_ROWS, 16), TEXT_ROWS), head]
             q = jnp.concatenate([q, words], axis=0)
+        scaled = q.astype(jnp.float32) * SCALE
+        high = scaled.astype(jnp.bfloat16)
+        low = (scaled - high.astype(jnp.float32)).astype(jnp.bfloat16)
+        q = jnp.concatenate([high, low], axis=1)
         t = lax.broadcasted_iota(jnp.int32, (1, CORES * TEXT_HERE), 1)
         position = (
             (lax.rem(t, TEXT_HERE) // TEXT_ROWS) * (CORES * TEXT_ROWS)
             + (t // TEXT_HERE) * TEXT_ROWS
             + lax.rem(t, TEXT_ROWS)
         )
-        scores = dot(q, text_keys[:, head], ((1,), (1,)))
+        words = text_keys[:, head]
+        scores = dot(q, jnp.concatenate([words, words], axis=1), ((1,), (1,)))
         scores = jnp.where(position < length[0], scores, NEG_BIG)
         ones = jnp.ones((CORES * TEXT_HERE, HEAD), jnp.bfloat16)
         block = jnp.concatenate([text_values[:, head], ones], axis=1)
@@ -214,12 +219,12 @@
                 following = dot(q, keys[h, lo : lo + PLANE, :], ((1,), (1,)))
             here = jnp.max(scores, axis=1, keepdims=True)
             new_top = here if top is None else jnp.maximum(top, here)
-            weights = jnp.exp2(scores * SCALE - new_top * SCALE).astype(jnp.bfloat16)
+            weights = jnp.exp2(scores - new_top).astype(jnp.bfloat16)
             product = dot(weights, block, ((1,), (0,)))
             if top is None:
                 summed = product
             else:
-                summed = summed * jnp.exp2((top - new_top) * SCALE) + product
+                summed = summed * jnp.exp2(top - new_top) + product
             top = new_top
             if lo < KEYS:
                 scores, block = following, values[h, lo : lo + PLANE, :]
@@ -315,6 +320,7 @@
                 rows = key_piece(1 - c, part)
                 wait_for(keys.at[h, rows, lanes], sib_recv.at[0, h, part])
                 wait_for(values.at[h, rows, lanes], sib_recv.at[1, h, part])
+            keys[h, :, HEAD:] = keys[h, :, :HEAD]
 
         @pl.when((i == XS - 2) & (h < HEADS_HERE - 1))
         def _():
@@ -415,7 +421,7 @@
         in_specs=[any_spec] * 7,
         out_specs=(vmem_spec, vmem_spec),
         scratch_shapes=[
-            pltpu.VMEM((HEADS_HERE, KEYS, HEAD), jnp.bfloat16),
+            pltpu.VMEM((HEADS_HERE, KEYS, 2 * HEAD), jnp.bfloat16),
             pltpu.VMEM((HEADS_HERE, KEYS, 2 * HEAD), jnp.bfloat16),
             pltpu.VMEM((HEADS_HERE, XS * VIDEO_PAIR, HEAD), jnp.bfloat16),
             pltpu.VMEM((HEADS_HERE, XS * PAIR, HEAD), jnp.bfloat16),

time: 82 us -> 81.9 us (level)
  no operation moved by 1% of the time
where the time goes in v6:
time: 81.9 us; the launch traced here: 81.1 us
  Pallas kernels  79.8 us (97%)
  between operations  1.29 us (2%)
    pallas_call x1, Pallas kernels, on_device(): pl.pallas_call(kernel, out_shape=out_shape, in_specs=[any_spec] * 7, out_...  78.6 us

profile of v6, /device:TPU:22, one launch (start us, length us, event | category | flops | bytes accessed | tf_op | source)
XLA Modules:
  0.0 81.1 jit_solution(12204000126089303144)
XLA Ops:
  1.3 78.6 %joint_attention.1 = (bf16[256,3072]{1,0:T(8,128)(2,1)S(1)}, bf16[16,3072]{1,0:T(8,128)(2,1)S(1)}) custom-call(s32[1]{0:T(128)S(6)} %copy.9.length_in, bf16[256,3072]{1,0:T(8,128)(2,1)} %vq.1, bf16[256,3072]{1,0:T(8,128)(2,1)} %vk.1, bf16[256,3072]{1,0:T(8,128)(2,1)} %vv.1, bf16[32,3072]{1,0:T(8,128)(2,1)} %tq.1, bf16[32,3072]{1,0:T(8,128)(2,1)} %tk.1, ...), custom_call_target="tpu_custom_call" | custom-call | flops 14545846272 | bytes 6291456 | tf_op jit(solution)/shard_map/joint_attention/pallas_call | solution.py:418
  79.9 1.2 %copy_out.1 = (bf16[256,3072]{1,0:T(8,128)(2,1)}, bf16[16,3072]{1,0:T(8,128)(2,1)}) custom-call(bf16[256,3072]{1,0:T(8,128)(2,1)S(1)} %get-tuple-element.4.video, bf16[16,3072]{1,0:T(8,128)(2,1)S(1)} %get-tuple-element.5.text), custom_call_target="tpu_custom_call" | custom-call | tf_op jit(solution)/shard_map/copy_out/pallas_call | solution.py:459
